TPU v7x, 512 devices: a whole 4x8x8 slice. The times are simulated.
512 devices in a mesh: seq: 32 (over z, x), req: 8 (over y), chan: 2 (over core).
Axes of the slice: x: 4, y: 8, z: 8, core: 2. Of those that a mesh axis runs over, the one named last changes fastest.
Arguments:
- context: bfloat16 [8, 4096, 4096], P('req', 'chan', 'seq'), may hold values from -6 to 6
- filters: bfloat16 [4096, 8192], P('chan', 'seq'), may hold values from -0.09375 to 0.09375
- lengths: int32 [8], replicated, may hold values from 131072 to 524288, as said below
Outputs:
- future: bfloat16 [8, 4096, 4096], P('req', 'chan', 'seq')
Inputs may be any that keep to these rules, and one draw needn't show every extreme that they name: `lengths`: exactly 4 of the 8 requests have a length that is a multiple of 4096; how many of them fall on one index of req differs between indices.
All inputs are finite; a program needn't handle non-finite values.
Results may differ from a plain program's by a relative error of at most 0.0078.
Values may be sent and summed in bfloat16 or wider, within the bound.
No kernel may reach another device: no remote copies, remote signals or barrier semaphores. Data moves between devices by JAX's collectives and lax.ppermute only.
A program may use at most 64 MiB of HBM per device.

v0:
```python
import math

import jax
import jax.numpy as jnp
from jax import lax
from jax.sharding import PartitionSpec as P

B = 4096


def trig_pair(first_count, second_count, stride_len, full_len):
    left_index = lax.broadcasted_iota(jnp.int32, (first_count, second_count), 0)
    right_index = lax.broadcasted_iota(jnp.int32, (first_count, second_count), 1)
    phases = left_index * right_index * stride_len % full_len
    angles = phases.astype(jnp.float32) * (2.0 * math.pi / full_len)
    return (jnp.cos(angles), jnp.sin(angles))


def trig_tables(row_count, col_count):
    full_len = row_count * col_count
    cos_rows, sin_rows = trig_pair(row_count, row_count, col_count, full_len)
    cos_turn, sin_turn = trig_pair(row_count, col_count, 1, full_len)
    cos_cols, sin_cols = trig_pair(col_count, col_count, row_count, full_len)
    return (
        cos_rows.astype(jnp.bfloat16),
        sin_rows.astype(jnp.bfloat16),
        cos_turn,
        sin_turn,
        cos_cols.astype(jnp.bfloat16),
        sin_cols.astype(jnp.bfloat16),
    )


def mat_cols(left_part, table):
    return jnp.dot(left_part, table, preferred_element_type=jnp.float32)


def mat_rows(table, right_part):
    return jnp.einsum("kp,...pq->...kq", table, right_part, preferred_element_type=jnp.float32)


def forward_spectrum(signal, trig):
    cos_rows, sin_rows, cos_turn, sin_turn, cos_cols, sin_cols = trig
    used_rows = signal.shape[-2]
    head_real = mat_rows(cos_rows[:, :used_rows], signal)
    head_imag = -mat_rows(sin_rows[:, :used_rows], signal)
    turn_real = (head_real * cos_turn + head_imag * sin_turn).astype(jnp.bfloat16)
    turn_imag = (head_imag * cos_turn - head_real * sin_turn).astype(jnp.bfloat16)
    spec_real = mat_cols(turn_real, cos_cols) + mat_cols(turn_imag, sin_cols)
    spec_imag = mat_cols(turn_imag, cos_cols) - mat_cols(turn_real, sin_cols)
    return (spec_real, spec_imag)


def future_block(signal, filter_spec, trig):
    cos_rows, sin_rows, cos_turn, sin_turn, cos_cols, sin_cols = trig
    spec_real, spec_imag = forward_spectrum(signal, trig)
    filt_real, filt_imag = filter_spec
    scale_inv = 1.0 / (cos_rows.shape[0] * cos_cols.shape[0])
    prod_real = ((spec_real * filt_real - spec_imag * filt_imag) * scale_inv).astype(jnp.bfloat16)
    prod_imag = ((spec_real * filt_imag + spec_imag * filt_real) * scale_inv).astype(jnp.bfloat16)
    back_real = mat_cols(prod_real, cos_cols) - mat_cols(prod_imag, sin_cols)
    back_imag = mat_cols(prod_real, sin_cols) + mat_cols(prod_imag, cos_cols)
    turn_real = (back_real * cos_turn - back_imag * sin_turn).astype(jnp.bfloat16)
    turn_imag = (back_real * sin_turn + back_imag * cos_turn).astype(jnp.bfloat16)
    half_rows = cos_rows.shape[0] // 2
    tail_real = mat_rows(cos_rows[half_rows:], turn_real)
    tail_imag = mat_rows(sin_rows[half_rows:], turn_imag)
    return (tail_real - tail_imag).astype(jnp.bfloat16)


def per_device(context, filters, lengths):
    seq_count = lax.axis_size("seq")
    home_index = lax.axis_index("req")
    per_req = context.shape[0]
    col_count = context.shape[2]
    row_count = 2 * seq_count
    trig = trig_tables(row_count, col_count)
    due_mask = lengths % B == 0
    lag_rows = lax.all_to_all(filters, "seq", split_axis=0, concat_axis=1, tiled=True)
    own_width = lag_rows.shape[0]
    filter_spec = forward_spectrum(lag_rows.reshape(own_width, row_count, col_count), trig)
    blocks = lax.all_to_all(context, "seq", split_axis=1, concat_axis=2, tiled=True)
    item_count = blocks.shape[0]
    signal = blocks.reshape(item_count, own_width, row_count // 2, col_count)
    future_part = future_block(signal, filter_spec, trig).reshape(item_count, own_width, -1)
    finished = lax.all_to_all(future_part, "seq", split_axis=2, concat_axis=1, tiled=True)
    local_due = lax.dynamic_slice_in_dim(due_mask, home_index * per_req, per_req)
    result = jnp.where(local_due[:, None, None], finished, 0)
    return result


def solution(mesh):
    in_specs = (P("req", "chan", "seq"), P("chan", "seq"), P())
    out_specs = P("req", "chan", "seq")
    return jax.shard_map(
        per_device, mesh=mesh, in_specs=in_specs, out_specs=out_specs, check_vma=False
    )
```

profile of v0, /device:TPU:32, one launch (start us, length us, event | category | flops | bytes accessed | tf_op | source)
XLA Modules:
  0.0 148.7 jit_solution(6187273489653464812)
XLA Ops:
  0.0 1.8 %copy.66 = bf16[1,2048,128]{2,0,1:T(2,128)(2,1)S(1)} copy(bf16[1,2048,128]{2,1,0:T(8,128)(2,1)} %param.3) | data formatting | bytes 1048576 | tf_op args[0]
  2.3 11.5 %reduce = bf16[2048,128]{1,0:T(8,128)(2,1)S(1)} reduce(bf16[2048,1,128]{2,1,0:T(2,128)(2,1)S(1)} %bitcast.136, bf16[]{:T(256)} %broadcast.224), dimensions={1}, to_apply=%bitcast.129.reduce_sub_computation | reduce | bytes 1048578
  14.0 30.7 %all_to_all.40 = bf16[32,2,4096]{2,1,0:T(2,128)(2,1)S(1)} all-to-all(bf16[32,2,4096]{2,1,0:T(2,128)(2,1)S(1)} %reshape.163), channel_id=1, replica_groups=mesh['seq'=32,'req'=8,'chan'=2] {'seq'}, dimensions={0} | all-to-all | bytes 1048576 | tf_op jit(solution)/shard_map/all_to_all | solution.py:82
  44.6 4.7 %all-to-all-start.1 = ((bf16[32,64,256]{2,1,0:T(8,128)(2,1)}), bf16[32,64,256]{2,1,0:T(8,128)(2,1)S(1)}, u32[]{:S(2)}, u32[]{:S(2)}) async-start(bf16[32,64,256]{2,1,0:T(8,128)(2,1)} %bitcast.21), calls=%async_computation.1 | async-start | bytes 2097152 | tf_op jit(solution)/shard_map/all_to_all | solution.py:79
  50.9 1.0 fusion.10
  52.6 2.0 %fusion.44 = f32[64,64,128]{2,1,0:T(8,128)} fusion(bf16[64,64,128]{2,1,0:T(8,128)(2,1)S(1)} %get-tuple-element.10), kind=kOutput, calls=%fused_computation.65 | convolution fusion | flops 134479872 | bytes 3145728 | tf_op jit(solution)/shard_map/dot_general | solution.py:35
  54.6 2.0 %convolution_add_fusion.2 = f32[64,64,128]{2,1,0:T(8,128)} fusion(f32[64,64,128]{2,1,0:T(8,128)S(1)} %fusion.48, bf16[64,64,128]{2,1,0:T(8,128)(2,1)S(1)} %get-tuple-element.10), kind=kOutput, calls=%fused_computation.20 | convolution fusion | flops 135004160 | bytes 5242880 | tf_op jit(solution)/shard_map/dot_general | solution.py:35
  56.6 19.9 %all-to-all-done.1 = bf16[32,64,256]{2,1,0:T(8,128)(2,1)S(1)} async-done(((bf16[32,64,256]{2,1,0:T(8,128)(2,1)}), bf16[32,64,256]{2,1,0:T(8,128)(2,1)S(1)}, u32[]{:S(2)}, u32[]{:S(2)}) %all-to-all-start.1) | async-done | bytes 1048608 | tf_op jit(solution)/shard_map/all_to_all | solution.py:79
  78.2 1.0 fusion.6
  79.9 0.7 fusion.46
  80.6 0.7 convolution_subtract_fusion.1
  82.0 0.9 copy-done
  83.5 1.2 multiply_convert_fusion
  86.1 0.7 convolution_subtract_fusion
  86.7 0.7 convolution_add_fusion
  88.7 2.8 %copy.42 = bf16[1,64,4096]{1,0,2:T(2,128)(2,1)S(1)} copy(bf16[1,64,4096]{2,1,0:T(8,128)(2,1)S(1)} %reshape.154) | data formatting | bytes 1048576 | tf_op jit(solution)/shard_map/reshape | solution.py:85
  91.5 22.6 %reduce.1 = bf16[4096,64]{1,0:T(8,128)(2,1)S(1)} reduce(bf16[4096,1,64]{2,1,0:T(2,128)(2,1)S(1)} %bitcast.131, bf16[]{:T(256)} %broadcast.224), dimensions={1}, to_apply=%bitcast.103.reduce_sub_computation | reduce | bytes 1048578
  114.2 1.5 %reshape.165 = bf16[32,2,4096]{2,1,0:T(2,128)(2,1)} reshape(bf16[4096,64]{1,0:T(8,128)(2,1)S(1)} %reduce.1) | data formatting | bytes 1048576
  115.7 5.6 %all-to-all-start.2 = ((bf16[32,2,4096]{2,1,0:T(2,128)(2,1)}), bf16[32,2,4096]{2,1,0:T(2,128)(2,1)S(1)}, u32[]{:S(2)}, u32[]{:S(2)}) async-start(bf16[32,2,4096]{2,1,0:T(2,128)(2,1)} %reshape.165), calls=%async_computation.2 | async-start | bytes 1048576 | tf_op jit(solution)/shard_map/all_to_all | solution.py:86
  121.9 16.0 %all-to-all-done.2 = bf16[32,2,4096]{2,1,0:T(2,128)(2,1)S(1)} async-done(((bf16[32,2,4096]{2,1,0:T(2,128)(2,1)}), bf16[32,2,4096]{2,1,0:T(2,128)(2,1)S(1)}, u32[]{:S(2)}, u32[]{:S(2)}) %all-to-all-start.2) | async-done | bytes 524320 | tf_op jit(solution)/shard_map/all_to_all | solution.py:86
  137.9 1.2 reshape.166
  139.1 3.9 %broadcast_select_fusion = bf16[1,64,4096]{1,0,2:T(2,128)(2,1)} fusion(pred[]{:T(512)} %bitcast, bf16[4096,1,64]{2,1,0:T(2,128)(2,1)S(1)} %reshape.166), kind=kLoop, calls=%fused_computation | loop fusion | flops 262144 | bytes 1048577 | tf_op jit(solution)/shard_map/jit(_where)/select_n | solution.py:88
  143.0 4.6 %copy.43 = bf16[1,64,4096]{2,1,0:T(8,128)(2,1)S(1)} copy(bf16[1,64,4096]{1,0,2:T(2,128)(2,1)} %broadcast_select_fusion) | data formatting | bytes 1048576 | tf_op jit(solution)/shard_map/jit(_where)/select_n | solution.py:88
  147.7 1.0 copy.44
  (28 shorter events, 9.9 us)
Async XLA Ops:
  44.6 31.8 %all-to-all-start.1 = ((bf16[32,64,256]{2,1,0:T(8,128)(2,1)}), bf16[32,64,256]{2,1,0:T(8,128)(2,1)S(1)}, u32[]{:S(2)}, u32[]{:S(2)}) async-start(bf16[32,64,256]{2,1,0:T(8,128)(2,1)} %bitcast.21), calls=%async_computation.1 | async-start | bytes 2097152 | tf_op jit(solution)/shard_map/all_to_all | solution.py:79
  81.3 1.6 %copy-start = (f32[64,64,128]{2,1,0:T(8,128)S(1)}, f32[64,64,128]{2,1,0:T(8,128)}, u32[]{:S(2)}) copy-start(f32[64,64,128]{2,1,0:T(8,128)} %fusion.44) | copy-start | bytes 6291460
  81.3 2.2 %copy-start.1 = (f32[64,64,128]{2,1,0:T(8,128)S(1)}, f32[64,64,128]{2,1,0:T(8,128)}, u32[]{:S(2)}) copy-start(f32[64,64,128]{2,1,0:T(8,128)} %convolution_add_fusion.2) | copy-start | bytes 6291460
  114.2 7.2 %copy-start.2 = (s32[8]{0:T(128)S(1)}, s32[8]{0:T(128)}, u32[]{:S(2)}) copy-start(s32[8]{0:T(128)} %param.5) | copy-start | bytes 100
  115.7 22.2 %all-to-all-start.2 = ((bf16[32,2,4096]{2,1,0:T(2,128)(2,1)}), bf16[32,2,4096]{2,1,0:T(2,128)(2,1)S(1)}, u32[]{:S(2)}, u32[]{:S(2)}) async-start(bf16[32,2,4096]{2,1,0:T(2,128)(2,1)} %reshape.165), calls=%async_computation.2 | async-start | bytes 1048576 | tf_op jit(solution)/shard_map/all_to_all | solution.py:86
where the time goes:
time: 149 us
  other arithmetic  38.5 us (26%)
  waiting for transfers between devices  35.8 us (24%)
  blocking collectives  30.7 us (21%)
  local copies, waits for them, and re-layouts  17.8 us (12%)
  matrix products  15.4 us (10%)
  starting transfers between devices  10.3 us (7%)
    unnamed x2, other arithmetic  34.2 us
    all_to_all x1, blocking collectives, per_device(): lax.all_to_all(context, 'seq', split_axis=1, concat_axis=2, tiled=True)  30.7 us
    all_to_all x1, waiting for transfers between devices, per_device(): lax.all_to_all(filters, 'seq', split_axis=0, concat_axis=1, tiled=True)  19.9 us
    all_to_all x1, waiting for transfers between devices, per_device(): lax.all_to_all(future_part, 'seq', split_axis=2, concat_axis=1, tiled=True)  16 us
    dot_general x12, matrix products, mat_cols(): return jnp.dot(left_part, table, preferred_element_type=jnp.float32)  11.2 us
    unnamed x14, local copies, waits for them, and re-layouts  7.44 us
    select_n x3, local copies, waits for them, and re-layouts, per_device(): result = jnp.where(local_due[:, None, None], finished, 0)  5.62 us
    all_to_all x1, starting transfers between devices, per_device(): lax.all_to_all(future_part, 'seq', split_axis=2, concat_axis=1, tiled=True)  5.59 us
  transfers between devices with their start and end apart: 2, of which 2 were waited for; matrix products, arithmetic and copies ran while one was open for 5% of the time, Pallas kernels for 0%

commit v1 on v0

v1 whole, which is shorter than its diff:
```python
import functools
import math

import jax
import jax.numpy as jnp
import numpy as np
from jax import lax
from jax.experimental import pallas as pl
from jax.experimental.pallas import tpu as pltpu
from jax.sharding import Mesh, PartitionSpec as P

B = 4096
C8 = 8


def trig_pair(first_count, second_count, stride_len, full_len):
    left = np.arange(first_count)[:, None]
    right = np.arange(second_count)[None, :]
    phases = (left * right * stride_len) % full_len
    angles = phases.astype(np.float64) * (2.0 * math.pi / full_len)
    return np.cos(angles).astype(np.float32), np.sin(angles).astype(np.float32)


def tables(rows, cols):
    full = rows * cols
    bf16 = jnp.bfloat16
    cp, sp = trig_pair(rows, rows, cols, full)
    ct, st = trig_pair(rows, cols, 1, full)
    cq, sq = trig_pair(cols, cols, rows, full)
    eye = np.eye(C8, dtype=np.float32)
    row_fwd = np.kron(np.concatenate([cp, -sp], 0), eye)
    half = rows // 2
    row_inv = np.kron(np.concatenate([cp[half:], -sp[half:]], 1), eye)
    col_fwd = np.block([[cq, -sq], [sq, cq]])
    col_inv = np.block([[cq, sq], [-sq, cq]])
    return (
        row_fwd.astype(bf16),
        row_inv.astype(bf16),
        col_fwd.astype(bf16),
        col_inv.astype(bf16),
        np.repeat(ct, C8, axis=0),
        np.repeat(st, C8, axis=0),
    )


def dot(a, b):
    return jnp.dot(a, b, preferred_element_type=jnp.float32)


def local_kernel(due_ref, got_ref, row_fwd, row_inv, col_fwd, col_inv, turn_cos, turn_sin, out_ref):
    seq, pair, rows, q = got_ref.shape
    chans = out_ref.shape[2]
    kc = turn_cos.shape[0]
    own = chans // pair
    scale = 1.0 / (2 * seq * q)
    ct, st = turn_cos[...], turn_sin[...]
    zero = jnp.zeros((seq, C8, q), jnp.float32)

    def spectrum(head):
        re, im = head[:kc], head[kc:]
        turned = jnp.concatenate(
            [
                (re * ct + im * st).astype(jnp.bfloat16),
                (im * ct - re * st).astype(jnp.bfloat16),
            ],
            1,
        )
        return dot(turned, col_fwd[...])

    def rows_of(part):
        return part.astype(jnp.float32).reshape(-1, q).astype(jnp.bfloat16)

    for group in range(chans // C8):
        holder, place = divmod(group * C8, own)
        first = chans + 2 * place
        taps = rows_of(got_ref[:, holder, first : first + 2 * C8, :])
        filt = spectrum(dot(row_fwd[...], taps)) * scale
        f_re, f_im = filt[:, :q], filt[:, q:]
        signal = jnp.concatenate(
            [rows_of(got_ref[:, b, group * C8 : (group + 1) * C8, :]) for b in range(pair)], 1
        )
        head = dot(row_fwd[:, : seq * C8], signal)
        back = []
        for b in range(pair):
            spec = spectrum(head[:, b * q : (b + 1) * q])
            s_re, s_im = spec[:, :q], spec[:, q:]
            prod = jnp.concatenate(
                [
                    (s_re * f_re - s_im * f_im).astype(jnp.bfloat16),
                    (s_re * f_im + s_im * f_re).astype(jnp.bfloat16),
                ],
                1,
            )
            u = dot(prod, col_inv[...])
            u_re, u_im = u[:, :q], u[:, q:]
            back.append(
                jnp.concatenate(
                    [
                        (u_re * ct - u_im * st).astype(jnp.bfloat16),
                        (u_re * st + u_im * ct).astype(jnp.bfloat16),
                    ],
                    0,
                )
            )
        tail = dot(row_inv[...], jnp.concatenate(back, 1))
        for b in range(pair):
            value = tail[:, b * q : (b + 1) * q].reshape(seq, C8, q)
            value = jnp.where(due_ref[b] == 0, value, zero)
            out_ref[:, b, group * C8 : (group + 1) * C8, :] = value.astype(jnp.bfloat16)


def per_device(consts, pair, context, filters, lengths):
    seq = lax.axis_size("seq")
    chans_all, q = context.shape[1], context.shape[2]
    peers = seq * pair
    chans = chans_all // peers
    own = chans // pair
    low = lax.axis_index("low")
    first = lax.axis_index("high") * pair
    left_over = lax.dynamic_slice_in_dim(lengths % B, first, pair)

    ctx = context.reshape(peers, chans, q)
    mine = lax.dynamic_index_in_dim(filters.reshape(peers, pair, own, 2 * q), low, 1, keepdims=False)
    parts = [ctx]
    for place in range(0, own, C8):
        for half in range(2):
            parts.append(mine[:, place : place + C8, half * q : (half + 1) * q])
    sent = jnp.concatenate(parts, 1)
    got = lax.all_to_all(sent, ("seq", "low"), split_axis=0, concat_axis=0)
    vmem = pl.BlockSpec(memory_space=pltpu.VMEM)
    out = pl.pallas_call(
        local_kernel,
        out_shape=jax.ShapeDtypeStruct((seq, pair, chans, q), jnp.bfloat16),
        in_specs=[pl.BlockSpec(memory_space=pltpu.SMEM)] + [vmem] * 7,
        out_specs=vmem,
        compiler_params=pltpu.CompilerParams(vmem_limit_bytes=48 << 20),
        name="transform",
    )(left_over, got.reshape(seq, pair, chans + 2 * own, q), *consts)
    home = lax.all_to_all(out.reshape(peers, chans, q), ("seq", "low"), split_axis=0, concat_axis=0)
    return home.reshape(context.shape)


def solution(mesh):
    seq, req, chan = (mesh.shape[a] for a in ("seq", "req", "chan"))
    pair = 2
    split = Mesh(mesh.devices.reshape(seq, req // pair, pair, chan), ("seq", "high", "low", "chan"))
    consts = tables(2 * seq, B // seq)
    spec = P(("high", "low"), "chan", "seq")
    return jax.shard_map(
        functools.partial(per_device, consts, pair),
        mesh=split,
        in_specs=(spec, P("chan", "seq"), P()),
        out_specs=spec,
        check_vma=False,
    )
```

time: 149 us -> 82.6 us (0.55)
  the two profiles are of different devices: /device:TPU:32 before, /device:TPU:16 now
where the time goes in v1:
time: 82.6 us; the launch traced here: 82.3 us
  waiting for transfers between devices  27.2 us (33%)
  blocking collectives  24.4 us (30%)
  starting transfers between devices  14.9 us (18%)
  local copies, waits for them, and re-layouts  9.28 us (11%)
  Pallas kernels  6.38 us (8%)
    all_to_all x1, waiting for transfers between devices, per_device(): got = lax.all_to_all(sent, ('seq', 'low'), split_axis=0, concat_axis=0)  27.2 us
    all_to_all x1, blocking collectives, per_device(): lax.all_to_all(out.reshape(peers, chans, q), ('seq', 'low'), split_axis=0...  24.4 us
    all_to_all x1, starting transfers between devices, per_device(): got = lax.all_to_all(sent, ('seq', 'low'), split_axis=0, concat_axis=0)  14.9 us
    unnamed x21, local copies, waits for them, and re-layouts  8.51 us
    pallas_call x1, Pallas kernels, per_device(): pl.pallas_call(local_kernel, out_shape=jax.ShapeDtypeStruct((seq, pair, c...  6.38 us
  transfers between devices with their start and end apart: 1, of which 1 were waited for; matrix products, arithmetic and copies ran while one was open for 0% of the time, Pallas kernels for 0%

profile of v1, /device:TPU:16, one launch (start us, length us, event | category | flops | bytes accessed | tf_op | source)
XLA Modules:
  0.0 82.3 jit_solution(11793251350388952885)
XLA Ops:
  0.0 0.0 copy-start
  0.0 2.1 %constant_dynamic-update-slice_fusion = bf16[64,64,128]{2,1,0:T(8,128)(2,1)} fusion(bf16[64,32,128]{2,1,0:T(8,128)(2,1)} %bitcast.11), kind=kLoop, calls=%fused_computation.5 | loop fusion | bytes 1048576
  2.1 0.0 copy-done
  2.1 0.7 slice_dynamic-update-slice_fusion.3
  2.8 0.7 slice_dynamic-update-slice_fusion.2
  3.5 0.7 slice_dynamic-update-slice_fusion.1
  4.2 0.7 slice_dynamic-update-slice_fusion
  4.9 0.0 copy-start.1
  4.9 0.0 copy-start.3
  4.9 14.9 %all-to-all-start = ((bf16[64,64,128]{2,1,0:T(8,128)(2,1)}), bf16[64,64,128]{2,1,0:T(8,128)(2,1)S(1)}, u32[]{:S(2)}, u32[]{:S(2)}) async-start(bf16[64,64,128]{2,1,0:T(8,128)(2,1)} %slice_dynamic-update-slice_fusion), calls=%async_computation | async-start | bytes 2097152 | tf_op jit(solution)/shard_map/all_to_all | solution.py:129
  19.8 0.0 copy-start.7
  19.8 0.6 copy-done.7
  20.5 0.1 dynamic_slice.7.due_ref
  20.6 27.2 %all-to-all-done = bf16[64,64,128]{2,1,0:T(8,128)(2,1)S(1)} async-done(((bf16[64,64,128]{2,1,0:T(8,128)(2,1)}), bf16[64,64,128]{2,1,0:T(8,128)(2,1)S(1)}, u32[]{:S(2)}, u32[]{:S(2)}) %all-to-all-start) | async-done | bytes 1048608 | tf_op jit(solution)/shard_map/all_to_all | solution.py:129
  47.8 0.0 copy-done.1
  47.8 0.0 copy-done.3
  47.8 0.0 copy-done.5
  47.8 0.0 copy-start.2
  47.8 1.0 %copy-done.2 = bf16[256,1024]{1,0:T(8,128)(2,1)S(1)} copy-done((bf16[256,1024]{1,0:T(8,128)(2,1)S(1)}, bf16[256,1024]{1,0:T(8,128)(2,1)}, u32[]{:S(2)}) %copy-start.2) | copy-done | bytes 524312
  48.8 0.9 %copy-done.4 = f32[512,128]{1,0:T(8,128)S(1)} copy-done((f32[512,128]{1,0:T(8,128)S(1)}, f32[512,128]{1,0:T(8,128)}, u32[]{:S(2)}) %copy-start.4) | copy-done | bytes 262168
  49.8 0.9 %copy-done.6 = bf16[256,256]{1,0:T(8,128)(2,1)S(1)} copy-done((bf16[256,256]{1,0:T(8,128)(2,1)S(1)}, bf16[256,256]{1,0:T(8,128)(2,1)}, u32[]{:S(2)}) %copy-start.6) | copy-done | bytes 131096
  50.7 6.4 %transform.1 = bf16[32,2,32,128]{3,2,1,0:T(8,128)(2,1)S(1)} custom-call(s32[2]{0:T(128)S(1)} %dynamic_slice.7.due_ref, bf16[32,2,64,128]{3,2,1,0:T(8,128)(2,1)S(1)} %bitcast.8, bf16[1024,512]{1,0:T(8,128)(2,1)S(1)} %copy-done.1, bf16[256,1024]{1,0:T(8,128)(2,1)S(1)} %copy-done.2, bf16[256,256]{1,0:T(8,128)(2,1)S(1)} %copy-done.6, ...), custom_call_target="tpu_custom_call" | custom-call | tf_op jit(solution)/shard_map/transform/pallas_call | solution.py:131
  57.1 24.4 %all_to_all.10 = bf16[64,32,128]{2,1,0:T(8,128)(2,1)S(1)} all-to-all(bf16[64,32,128]{2,1,0:T(8,128)(2,1)S(1)} %bitcast.9), channel_id=1, replica_groups=mesh['seq'=32,'high'=4,'low'=2,'chan'=2] {'seq','low'}, dimensions={0} | all-to-all | bytes 1048576 | tf_op jit(solution)/shard_map/all_to_all | solution.py:139
  81.5 0.8 copy.15
  (5 shorter events, 0.0 us)
Async XLA Ops:
  0.0 2.1 %copy-start = (bf16[2048,256]{1,0:T(8,128)(2,1)S(1)}, bf16[2048,256]{1,0:T(8,128)(2,1)}, u32[]{:S(2)}) copy-start(bf16[2048,256]{1,0:T(8,128)(2,1)} %param.10) | copy-start | bytes 3145732
  4.9 42.9 %copy-start.1 = (bf16[1024,512]{1,0:T(8,128)(2,1)S(1)}, bf16[1024,512]{1,0:T(8,128)(2,1)}, u32[]{:S(2)}) copy-start(bf16[1024,512]{1,0:T(8,128)(2,1)} %constant.45.clone.row_fwd) | copy-start | bytes 3145732
  4.9 42.9 %copy-start.3 = (f32[512,128]{1,0:T(8,128)S(1)}, f32[512,128]{1,0:T(8,128)}, u32[]{:S(2)}) copy-start(f32[512,128]{1,0:T(8,128)} %constant.50.clone.turn_sin) | copy-start | bytes 786436
  4.9 42.9 %copy-start.5 = (bf16[256,256]{1,0:T(8,128)(2,1)S(1)}, bf16[256,256]{1,0:T(8,128)(2,1)}, u32[]{:S(2)}) copy-start(bf16[256,256]{1,0:T(8,128)(2,1)} %constant.48.clone.col_inv) | copy-start | bytes 393220
  4.9 42.9 %all-to-all-start = ((bf16[64,64,128]{2,1,0:T(8,128)(2,1)}), bf16[64,64,128]{2,1,0:T(8,128)(2,1)S(1)}, u32[]{:S(2)}, u32[]{:S(2)}) async-start(bf16[64,64,128]{2,1,0:T(8,128)(2,1)} %slice_dynamic-update-slice_fusion), calls=%async_computation | async-start | bytes 2097152 | tf_op jit(solution)/shard_map/all_to_all | solution.py:129
  19.8 0.7 copy-start.7
  47.8 1.0 %copy-start.2 = (bf16[256,1024]{1,0:T(8,128)(2,1)S(1)}, bf16[256,1024]{1,0:T(8,128)(2,1)}, u32[]{:S(2)}) copy-start(bf16[256,1024]{1,0:T(8,128)(2,1)} %constant.46.clone.row_inv) | copy-start | bytes 1572868
  48.8 0.9 %copy-start.4 = (f32[512,128]{1,0:T(8,128)S(1)}, f32[512,128]{1,0:T(8,128)}, u32[]{:S(2)}) copy-start(f32[512,128]{1,0:T(8,128)} %constant.49.clone.turn_cos) | copy-start | bytes 786436
  49.8 0.9 %copy-start.6 = (bf16[256,256]{1,0:T(8,128)(2,1)S(1)}, bf16[256,256]{1,0:T(8,128)(2,1)}, u32[]{:S(2)}) copy-start(bf16[256,256]{1,0:T(8,128)(2,1)} %constant.47.clone.col_fwd) | copy-start | bytes 393220

commit v2 on v1

v2 whole, which is shorter than its diff:
```python
import functools
import math

import jax
import jax.numpy as jnp
import numpy as np
from jax import lax
from jax.experimental import pallas as pl
from jax.experimental.pallas import tpu as pltpu
from jax.sharding import Mesh, PartitionSpec as P

B = 4096
C8 = 8


def trig_pair(first_count, second_count, stride_len, full_len):
    left = np.arange(first_count)[:, None]
    right = np.arange(second_count)[None, :]
    phases = (left * right * stride_len) % full_len
    angles = phases.astype(np.float64) * (2.0 * math.pi / full_len)
    return np.cos(angles).astype(np.float32), np.sin(angles).astype(np.float32)


def tables(rows, cols):
    full = rows * cols
    cp, sp = trig_pair(rows, rows, cols, full)
    ct, st = trig_pair(rows, cols, 1, full)
    cq, sq = trig_pair(cols, cols, rows, full)
    eye = np.eye(C8, dtype=np.float32)
    half = rows // 2
    row_fwd = np.kron(np.concatenate([cp, -sp], 0), eye)
    row_inv = np.concatenate([np.kron(cp[half:], eye), np.kron(-sp[half:], eye)], 0)
    col = np.concatenate([np.block([[cq, -sq], [sq, cq]]), np.block([[cq, sq], [-sq, cq]])], 1)
    bands = np.concatenate([row_fwd, row_inv, col], 0).astype(jnp.bfloat16)
    turn = np.repeat(np.concatenate([ct, st], 1), C8, axis=0)
    return bands, turn


def dot(a, b):
    return jnp.dot(a, b, preferred_element_type=jnp.float32)


def pack_kernel(low_ref, context_ref, filters_ref, sent_ref, sems):
    chans, q = context_ref.shape[1:]
    own = filters_ref.shape[2]
    low = low_ref[0]
    copies = [pltpu.make_async_copy(context_ref, sent_ref.at[:, pl.ds(0, chans), :], sems.at[0])]
    for half in range(2):
        copies.append(
            pltpu.make_async_copy(
                filters_ref.at[:, low, :, pl.ds(half * q, q)],
                sent_ref.at[:, pl.ds(chans + half * own, own), :],
                sems.at[1 + half],
            )
        )
    for copy in copies:
        copy.start()
    for copy in copies:
        copy.wait()


def local_kernel(due_ref, got_ref, bands_ref, turn_ref, out_ref):
    seq, pair, rows, q = got_ref.shape
    chans = out_ref.shape[2]
    own = chans // pair
    kc = turn_ref.shape[0]
    row_fwd = bands_ref.at[pl.ds(0, 2 * kc), :]
    row_inv = bands_ref.at[pl.ds(2 * kc, kc), :]
    col = bands_ref.at[pl.ds(3 * kc, 2 * q), :]
    groups = chans // C8
    scale = 1.0 / (2 * seq * q)
    ct, st = turn_ref[:, :q], turn_ref[:, q:]
    zero = jnp.zeros((seq, C8, q), jnp.float32)

    def narrow(part):
        return part.astype(jnp.bfloat16)

    def spectrum(head):
        re, im = head[:kc], head[kc:]
        turned = jnp.concatenate([narrow(re * ct + im * st), narrow(im * ct - re * st)], 1)
        return dot(turned, col[:, : 2 * q])

    taps = []
    for group in range(groups):
        holder, place = divmod(group * C8, own)
        halves = [
            got_ref[:, holder, chans + half * own + place : chans + half * own + place + C8, :].astype(jnp.float32)
            for half in range(2)
        ]
        taps.append(narrow(jnp.stack(halves, 1).reshape(2 * seq * C8, q)))
    filt = []
    for group in range(0, groups, 2):
        head = dot(row_fwd[...], jnp.concatenate(taps[group : group + 2], 1))
        for k in range(2):
            filt.append(spectrum(head[:, k * q : (k + 1) * q]) * scale)

    for group in range(groups):
        f_re, f_im = filt[group][:, :q], filt[group][:, q:]
        lanes = pl.ds(group * C8, C8)
        signal = [narrow(got_ref[:, b, lanes, :].astype(jnp.float32).reshape(seq * C8, q)) for b in range(pair)]
        head = dot(row_fwd[:, : seq * C8], jnp.concatenate(signal, 1))
        back_re, back_im = [], []
        for b in range(pair):
            spec = spectrum(head[:, b * q : (b + 1) * q])
            s_re, s_im = spec[:, :q], spec[:, q:]
            prod = jnp.concatenate([narrow(s_re * f_re - s_im * f_im), narrow(s_re * f_im + s_im * f_re)], 1)
            u = dot(prod, col[:, 2 * q :])
            u_re, u_im = u[:, :q], u[:, q:]
            back_re.append(narrow(u_re * ct - u_im * st))
            back_im.append(narrow(u_re * st + u_im * ct))
        half = seq * C8
        tail = dot(row_inv[:half], jnp.concatenate(back_re, 1)) + dot(row_inv[half:], jnp.concatenate(back_im, 1))
        for b in range(pair):
            value = tail[:, b * q : (b + 1) * q].reshape(seq, C8, q)
            value = jnp.where(due_ref[b] == 0, value, zero)
            out_ref[:, b, lanes, :] = narrow(value)


def per_device(consts, pair, context, filters, lengths):
    seq = lax.axis_size("seq")
    chans_all, q = context.shape[1], context.shape[2]
    peers = seq * pair
    chans = chans_all // peers
    own = chans // pair
    rows = chans + 2 * own
    low = lax.axis_index("low")
    first = lax.axis_index("high") * pair
    left_over = lax.dynamic_slice_in_dim(lengths % B, first, pair)
    smem = pl.BlockSpec(memory_space=pltpu.SMEM)
    vmem = pl.BlockSpec(memory_space=pltpu.VMEM)
    anyw = pl.BlockSpec(memory_space=pl.ANY)

    sent = pl.pallas_call(
        pack_kernel,
        out_shape=jax.ShapeDtypeStruct((peers, rows, q), jnp.bfloat16),
        in_specs=[smem, anyw, anyw],
        out_specs=anyw,
        scratch_shapes=[pltpu.SemaphoreType.DMA((3,))],
        name="pack",
    )(low[None], context.reshape(peers, chans, q), filters.reshape(peers, pair, own, 2 * q))
    got = lax.all_to_all(sent, ("seq", "low"), split_axis=0, concat_axis=0)
    out = pl.pallas_call(
        local_kernel,
        out_shape=jax.ShapeDtypeStruct((seq, pair, chans, q), jnp.bfloat16),
        in_specs=[smem] + [vmem] * 3,
        out_specs=vmem,
        compiler_params=pltpu.CompilerParams(vmem_limit_bytes=48 << 20),
        name="transform",
    )(left_over, got.reshape(seq, pair, rows, q), *consts)
    home = lax.all_to_all(out.reshape(peers, chans, q), ("seq", "low"), split_axis=0, concat_axis=0)
    return home.reshape(context.shape)


def solution(mesh):
    seq, req, chan = (mesh.shape[a] for a in ("seq", "req", "chan"))
    pair = 2
    split = Mesh(mesh.devices.reshape(seq, req // pair, pair, chan), ("seq", "high", "low", "chan"))
    consts = tables(2 * seq, B // seq)
    spec = P(("high", "low"), "chan", "seq")
    return jax.shard_map(
        functools.partial(per_device, consts, pair),
        mesh=split,
        in_specs=(spec, P("chan", "seq"), P()),
        out_specs=spec,
        check_vma=False,
    )
```

time: 82.6 us -> 107 us (1.30)
  Pallas kernels: 6.38 us -> 38.3 us
  local copies, waits for them, and re-layouts: 9.28 us -> 0.88 us
    pallas_call x0 -> x1, Pallas kernels: none -> 32.9 us  [per_device(): pl.pallas_call(pack_kernel, out_shape=jax.ShapeDtypeStruct((peers, rows,...]
    unnamed x21 -> x7, local copies, waits for them, and re-layouts: 8.51 us -> 0.8 us
where the time goes in v2:
time: 107 us; the launch traced here: 106 us
  Pallas kernels  38.3 us (36%)
  waiting for transfers between devices  27.9 us (26%)
  blocking collectives  24.4 us (23%)
  starting transfers between devices  14.8 us (14%)
    pallas_call x1, Pallas kernels, per_device(): pl.pallas_call(pack_kernel, out_shape=jax.ShapeDtypeStruct((peers, rows,...  32.9 us
    all_to_all x1, waiting for transfers between devices, per_device(): got = lax.all_to_all(sent, ('seq', 'low'), split_axis=0, concat_axis=0)  27.9 us
    all_to_all x1, blocking collectives, per_device(): lax.all_to_all(out.reshape(peers, chans, q), ('seq', 'low'), split_axis=0...  24.4 us
    all_to_all x1, starting transfers between devices, per_device(): got = lax.all_to_all(sent, ('seq', 'low'), split_axis=0, concat_axis=0)  14.8 us
    pallas_call x1, Pallas kernels, per_device(): pl.pallas_call(local_kernel, out_shape=jax.ShapeDtypeStruct((seq, pair, c...  5.42 us
  transfers between devices with their start and end apart: 1, of which 1 were waited for; matrix products, arithmetic and copies ran while one was open for 0% of the time, Pallas kernels for 0%

profile of v2, /device:TPU:16, one launch (start us, length us, event | category | flops | bytes accessed | tf_op | source)
XLA Modules:
  0.0 106.3 jit_solution(1683283627686170066)
XLA Ops:
  0.0 0.0 copy-start.2
  0.0 0.0 copy-start
  0.0 0.0 copy-start.1
  0.0 32.9 %pack.1 = bf16[64,64,128]{2,1,0:T(8,128)(2,1)} custom-call(s32[1]{0:T(128)} %bitcast.low_ref, bf16[64,32,128]{2,1,0:T(8,128)(2,1)} %bitcast.10, bf16[64,2,16,256]{3,2,1,0:T(8,128)(2,1)} %bitcast.9), custom_call_target="tpu_custom_call" | custom-call | tf_op jit(solution)/shard_map/pack/pallas_call | solution.py:133
  32.9 14.8 %all-to-all-start = ((bf16[64,64,128]{2,1,0:T(8,128)(2,1)}), bf16[64,64,128]{2,1,0:T(8,128)(2,1)S(1)}, u32[]{:S(2)}, u32[]{:S(2)}) async-start(bf16[64,64,128]{2,1,0:T(8,128)(2,1)} %pack.1), calls=%async_computation | async-start | bytes 2097152 | tf_op jit(solution)/shard_map/all_to_all | solution.py:141
  47.7 0.0 copy-done.2
  47.8 0.1 dynamic_slice.3.due_ref
  47.8 27.9 %all-to-all-done = bf16[64,64,128]{2,1,0:T(8,128)(2,1)S(1)} async-done(((bf16[64,64,128]{2,1,0:T(8,128)(2,1)}), bf16[64,64,128]{2,1,0:T(8,128)(2,1)S(1)}, u32[]{:S(2)}, u32[]{:S(2)}) %all-to-all-start) | async-done | bytes 1048608 | tf_op jit(solution)/shard_map/all_to_all | solution.py:141
  75.7 0.0 copy-done
  75.7 0.0 copy-done.1
  75.7 5.4 %transform.1 = bf16[32,2,32,128]{3,2,1,0:T(8,128)(2,1)S(1)} custom-call(s32[2]{0:T(128)S(1)} %dynamic_slice.3.due_ref, bf16[32,2,64,128]{3,2,1,0:T(8,128)(2,1)S(1)} %bitcast.6, bf16[1792,512]{1,0:T(8,128)(2,1)S(1)} %copy-done, f32[512,256]{1,0:T(8,128)S(1)} %copy-done.1), custom_call_target="tpu_custom_call" | custom-call | tf_op jit(solution)/shard_map/transform/pallas_call | solution.py:142
  81.1 24.4 %all_to_all.10 = bf16[64,32,128]{2,1,0:T(8,128)(2,1)S(1)} all-to-all(bf16[64,32,128]{2,1,0:T(8,128)(2,1)S(1)} %bitcast.7), channel_id=1, replica_groups=mesh['seq'=32,'high'=4,'low'=2,'chan'=2] {'seq','low'}, dimensions={0} | all-to-all | bytes 1048576 | tf_op jit(solution)/shard_map/all_to_all | solution.py:150
  105.6 0.8 copy.7
  (1 shorter events, 0.0 us)
Async XLA Ops:
  0.0 47.7 %copy-start.2 = (s32[8]{0:T(128)S(1)}, s32[8]{0:T(128)}, u32[]{:S(2)}) copy-start(s32[8]{0:T(128)} %param.7) | copy-start | bytes 100
  0.0 75.7 %copy-start = (bf16[1792,512]{1,0:T(8,128)(2,1)S(1)}, bf16[1792,512]{1,0:T(8,128)(2,1)}, u32[]{:S(2)}) copy-start(bf16[1792,512]{1,0:T(8,128)(2,1)} %constant.33.clone.bands_ref) | copy-start | bytes 5505028
  0.0 75.7 %copy-start.1 = (f32[512,256]{1,0:T(8,128)S(1)}, f32[512,256]{1,0:T(8,128)}, u32[]{:S(2)}) copy-start(f32[512,256]{1,0:T(8,128)} %constant.34.clone.turn_ref) | copy-start | bytes 1572868
  32.9 42.8 %all-to-all-start = ((bf16[64,64,128]{2,1,0:T(8,128)(2,1)}), bf16[64,64,128]{2,1,0:T(8,128)(2,1)S(1)}, u32[]{:S(2)}, u32[]{:S(2)}) async-start(bf16[64,64,128]{2,1,0:T(8,128)(2,1)} %pack.1), calls=%async_computation | async-start | bytes 2097152 | tf_op jit(solution)/shard_map/all_to_all | solution.py:141

commit v3 on v2

v3 whole, which is shorter than its diff:
```python
import functools
import math

import jax
import jax.numpy as jnp
import numpy as np
from jax import lax
from jax.experimental import pallas as pl
from jax.experimental.pallas import tpu as pltpu
from jax.sharding import Mesh, PartitionSpec as P

B = 4096
C8 = 8


def trig_pair(first_count, second_count, stride_len, full_len):
    left = np.arange(first_count)[:, None]
    right = np.arange(second_count)[None, :]
    phases = (left * right * stride_len) % full_len
    angles = phases.astype(np.float64) * (2.0 * math.pi / full_len)
    return np.cos(angles).astype(np.float32), np.sin(angles).astype(np.float32)


def tables(rows, cols):
    full = rows * cols
    half = rows // 2
    cp, sp = trig_pair(rows, rows, cols, full)
    ct, st = trig_pair(rows, cols, 1, full)
    cq, sq = trig_pair(cols, cols, rows, full)
    eye = np.eye(C8, dtype=np.float32)
    row_fwd = np.kron(np.concatenate([cp[: half + 1], -sp[1:half]], 0), eye)
    twice = np.where(np.arange(half + 1) % half == 0, 1.0, 2.0) / full
    back = np.concatenate([cp[half:, : half + 1] * twice, -sp[half:, 1:half] * twice[1:half]], 1)
    row_inv = np.kron(back, eye)
    col = np.concatenate([np.block([[cq, -sq], [sq, cq]]), np.block([[cq, sq], [-sq, cq]])], 1)
    bands = np.concatenate([row_fwd, row_inv, col], 0).astype(jnp.bfloat16)
    turn = np.repeat(np.concatenate([ct, st], 1)[: half + 1], C8, axis=0).astype(np.float32)
    return bands, turn


def dot(a, b):
    return jnp.dot(a, b, preferred_element_type=jnp.float32)


def pack_kernel(low_ref, context_ref, filters_ref, sent_ref):
    chans, q = context_ref.shape[1:]
    own = filters_ref.shape[2]
    sent_ref[:, :chans, :] = context_ref[...]
    for half in range(2):
        sent_ref[:, chans + half * own : chans + (half + 1) * own, :] = filters_ref[:, 0, :, half * q : (half + 1) * q]


def local_kernel(due_ref, got_ref, bands_ref, turn_ref, out_ref):
    seq, pair, rows, q = got_ref.shape
    chans = out_ref.shape[2]
    own = chans // pair
    length = 2 * seq * C8
    kept = turn_ref.shape[0]
    row_fwd = bands_ref.at[pl.ds(0, length), :]
    row_inv = bands_ref.at[pl.ds(length, length // 2), :]
    col = bands_ref.at[pl.ds(length + length // 2, 2 * q), :]
    groups = chans // C8
    ct, st = turn_ref[:, :q], turn_ref[:, q:]
    edge = jnp.zeros((C8, q), jnp.float32)
    zero = jnp.zeros((seq, C8, q), jnp.float32)

    def narrow(part):
        return part.astype(jnp.bfloat16)

    def spectra(head):
        turned = []
        for i in range(head.shape[1] // q):
            part = head[:, i * q : (i + 1) * q]
            re = part[:kept]
            im = jnp.concatenate([edge, part[kept:], edge], 0)
            turned.append(jnp.concatenate([re * ct + im * st, im * ct - re * st], 1))
        return dot(narrow(jnp.concatenate(turned, 0)), col[:, : 2 * q])

    taps = []
    for group in range(groups):
        holder, place = divmod(group * C8, own)
        halves = [
            got_ref[:, holder, chans + half * own + place : chans + half * own + place + C8, :].astype(jnp.float32)
            for half in range(2)
        ]
        taps.append(narrow(jnp.stack(halves, 1).reshape(length, q)))
    filt = []
    for group in range(0, groups, 2):
        both = spectra(dot(row_fwd[...], jnp.concatenate(taps[group : group + 2], 1)))
        filt += [both[:kept], both[kept:]]

    for group in range(groups):
        f_re, f_im = filt[group][:, :q], filt[group][:, q:]
        lanes = pl.ds(group * C8, C8)
        signal = [narrow(got_ref[:, b, lanes, :].astype(jnp.float32).reshape(seq * C8, q)) for b in range(pair)]
        spec = spectra(dot(row_fwd[:, : seq * C8], jnp.concatenate(signal, 1)))
        prod = []
        for b in range(pair):
            s_re, s_im = spec[b * kept : (b + 1) * kept, :q], spec[b * kept : (b + 1) * kept, q:]
            prod.append(jnp.concatenate([s_re * f_re - s_im * f_im, s_re * f_im + s_im * f_re], 1))
        u = dot(narrow(jnp.concatenate(prod, 0)), col[:, 2 * q :])
        back = []
        for b in range(pair):
            u_re, u_im = u[b * kept : (b + 1) * kept, :q], u[b * kept : (b + 1) * kept, q:]
            v_im = u_re * st + u_im * ct
            back.append(jnp.concatenate([u_re * ct - u_im * st, v_im[C8 : kept - C8]], 0))
        tail = dot(row_inv[...], narrow(jnp.concatenate(back, 1)))
        for b in range(pair):
            value = tail[:, b * q : (b + 1) * q].reshape(seq, C8, q)
            value = jnp.where(due_ref[b] == 0, value, zero)
            out_ref[:, b, lanes, :] = narrow(value)


def per_device(consts, pair, context, filters, lengths):
    seq = lax.axis_size("seq")
    chans_all, q = context.shape[1], context.shape[2]
    peers = seq * pair
    chans = chans_all // peers
    own = chans // pair
    rows = chans + 2 * own
    low = lax.axis_index("low")
    first = lax.axis_index("high") * pair
    left_over = lax.dynamic_slice_in_dim(lengths % B, first, pair)
    smem = pl.BlockSpec(memory_space=pltpu.SMEM)
    vmem = pl.BlockSpec(memory_space=pltpu.VMEM)

    steps = 2
    part = peers // steps
    sent = pl.pallas_call(
        pack_kernel,
        out_shape=jax.ShapeDtypeStruct((peers, rows, q), jnp.bfloat16),
        grid_spec=pltpu.PrefetchScalarGridSpec(
            num_scalar_prefetch=1,
            grid=(steps,),
            in_specs=[
                pl.BlockSpec((part, chans, q), lambda i, low_ref: (i, 0, 0)),
                pl.BlockSpec((part, 1, own, 2 * q), lambda i, low_ref: (i, low_ref[0], 0, 0)),
            ],
            out_specs=pl.BlockSpec((part, rows, q), lambda i, low_ref: (i, 0, 0)),
        ),
        name="pack",
    )(low[None], context.reshape(peers, chans, q), filters.reshape(peers, pair, own, 2 * q))
    got = lax.all_to_all(sent, ("seq", "low"), split_axis=0, concat_axis=0)
    out = pl.pallas_call(
        local_kernel,
        out_shape=jax.ShapeDtypeStruct((seq, pair, chans, q), jnp.bfloat16),
        in_specs=[smem] + [vmem] * 3,
        out_specs=vmem,
        compiler_params=pltpu.CompilerParams(vmem_limit_bytes=48 << 20),
        name="transform",
    )(left_over, got.reshape(seq, pair, rows, q), *consts)
    home = lax.all_to_all(out.reshape(peers, chans, q), ("seq", "low"), split_axis=0, concat_axis=0)
    return home.reshape(context.shape)


def solution(mesh):
    seq, req, chan = (mesh.shape[a] for a in ("seq", "req", "chan"))
    pair = 2
    split = Mesh(mesh.devices.reshape(seq, req // pair, pair, chan), ("seq", "high", "low", "chan"))
    consts = tables(2 * seq, B // seq)
    spec = P(("high", "low"), "chan", "seq")
    return jax.shard_map(
        functools.partial(per_device, consts, pair),
        mesh=split,
        in_specs=(spec, P("chan", "seq"), P()),
        out_specs=spec,
        check_vma=False,
    )
```

time: 107 us -> 74.4 us (0.70)
  Pallas kernels: 38.3 us -> 5.95 us
    pallas_call x1, Pallas kernels: 32.9 us -> 2.07 us  [per_device(): pl.pallas_call(pack_kernel, out_shape=jax.ShapeDtypeStruct((peers, rows,...]
    pallas_call x1, Pallas kernels: 5.42 us -> 3.89 us  [per_device(): pl.pallas_call(local_kernel, out_shape=jax.ShapeDtypeStruct((seq, pair, c...]
where the time goes in v3:
time: 74.4 us; the launch traced here: 74.1 us
  waiting for transfers between devices  27.2 us (37%)
  blocking collectives  24.4 us (33%)
  starting transfers between devices  14.9 us (20%)
  Pallas kernels  5.95 us (8%)
  local copies, waits for them, and re-layouts  1.53 us (2%)
    all_to_all x1, waiting for transfers between devices, per_device(): got = lax.all_to_all(sent, ('seq', 'low'), split_axis=0, concat_axis=0)  27.2 us
    all_to_all x1, blocking collectives, per_device(): lax.all_to_all(out.reshape(peers, chans, q), ('seq', 'low'), split_axis=0...  24.4 us
    all_to_all x1, starting transfers between devices, per_device(): got = lax.all_to_all(sent, ('seq', 'low'), split_axis=0, concat_axis=0)  14.9 us
    pallas_call x1, Pallas kernels, per_device(): pl.pallas_call(local_kernel, out_shape=jax.ShapeDtypeStruct((seq, pair, c...  3.89 us
    pallas_call x1, Pallas kernels, per_device(): pl.pallas_call(pack_kernel, out_shape=jax.ShapeDtypeStruct((peers, rows,...  2.07 us
  transfers between devices with their start and end apart: 1, of which 1 were waited for; matrix products, arithmetic and copies ran while one was open for 0% of the time, Pallas kernels for 0%

profile of v3, /device:TPU:16, one launch (start us, length us, event | category | flops | bytes accessed | tf_op | source)
XLA Modules:
  0.0 74.1 jit_solution(12298036146469758374)
XLA Ops:
  0.0 2.1 %pack.1 = bf16[64,64,128]{2,1,0:T(8,128)(2,1)} custom-call(s32[1]{0:T(128)} %bitcast.low_ref, bf16[64,32,128]{2,1,0:T(8,128)(2,1)} %bitcast.10, bf16[64,2,16,256]{3,2,1,0:T(8,128)(2,1)} %bitcast.9), custom_call_target="tpu_custom_call" | custom-call | tf_op jit(solution)/shard_map/pack/pallas_call | solution.py:129
  2.1 0.0 copy-start
  2.1 0.0 copy-start.1
  2.1 14.9 %all-to-all-start = ((bf16[64,64,128]{2,1,0:T(8,128)(2,1)}), bf16[64,64,128]{2,1,0:T(8,128)(2,1)S(1)}, u32[]{:S(2)}, u32[]{:S(2)}) async-start(bf16[64,64,128]{2,1,0:T(8,128)(2,1)} %pack.1), calls=%async_computation | async-start | bytes 2097152 | tf_op jit(solution)/shard_map/all_to_all | solution.py:143
  17.0 0.0 copy-start.2
  17.0 0.6 copy-done.2
  17.7 0.1 dynamic_slice.3.due_ref
  17.8 27.2 %all-to-all-done = bf16[64,64,128]{2,1,0:T(8,128)(2,1)S(1)} async-done(((bf16[64,64,128]{2,1,0:T(8,128)(2,1)}), bf16[64,64,128]{2,1,0:T(8,128)(2,1)S(1)}, u32[]{:S(2)}, u32[]{:S(2)}) %all-to-all-start) | async-done | bytes 1048608 | tf_op jit(solution)/shard_map/all_to_all | solution.py:143
  45.0 0.0 copy-done
  45.0 0.0 copy-done.1
  45.0 3.9 %transform.1 = bf16[32,2,32,128]{3,2,1,0:T(8,128)(2,1)S(1)} custom-call(s32[2]{0:T(128)S(1)} %dynamic_slice.3.due_ref, bf16[32,2,64,128]{3,2,1,0:T(8,128)(2,1)S(1)} %bitcast.6, bf16[1024,512]{1,0:T(8,128)(2,1)S(1)} %copy-done, f32[264,256]{1,0:T(8,128)S(1)} %copy-done.1), custom_call_target="tpu_custom_call" | custom-call | tf_op jit(solution)/shard_map/transform/pallas_call | solution.py:144
  48.9 24.4 %all_to_all.10 = bf16[64,32,128]{2,1,0:T(8,128)(2,1)S(1)} all-to-all(bf16[64,32,128]{2,1,0:T(8,128)(2,1)S(1)} %bitcast.7), channel_id=1, replica_groups=mesh['seq'=32,'high'=4,'low'=2,'chan'=2] {'seq','low'}, dimensions={0} | all-to-all | bytes 1048576 | tf_op jit(solution)/shard_map/all_to_all | solution.py:152
  73.3 0.8 %copy.7 = bf16[1,2048,128]{2,1,0:T(8,128)(2,1)} copy(bf16[1,2048,128]{2,1,0:T(8,128)(2,1)S(1)} %bitcast.8) | data formatting | bytes 1048576
  (1 shorter events, 0.0 us)
Async XLA Ops:
  2.1 42.9 %copy-start = (bf16[1024,512]{1,0:T(8,128)(2,1)S(1)}, bf16[1024,512]{1,0:T(8,128)(2,1)}, u32[]{:S(2)}) copy-start(bf16[1024,512]{1,0:T(8,128)(2,1)} %constant.33.clone.bands_ref) | copy-start | bytes 3145732
  2.1 42.9 %copy-start.1 = (f32[264,256]{1,0:T(8,128)S(1)}, f32[264,256]{1,0:T(8,128)}, u32[]{:S(2)}) copy-start(f32[264,256]{1,0:T(8,128)} %constant.34.clone.turn_ref) | copy-start | bytes 811012
  2.1 42.9 %all-to-all-start = ((bf16[64,64,128]{2,1,0:T(8,128)(2,1)}), bf16[64,64,128]{2,1,0:T(8,128)(2,1)S(1)}, u32[]{:S(2)}, u32[]{:S(2)}) async-start(bf16[64,64,128]{2,1,0:T(8,128)(2,1)} %pack.1), calls=%async_computation | async-start | bytes 2097152 | tf_op jit(solution)/shard_map/all_to_all | solution.py:143
  17.0 0.7 copy-start.2

commit v4 on v3

v4 whole, which is shorter than its diff:
```python
import functools
import math

import jax
import jax.numpy as jnp
import numpy as np
from jax import lax
from jax.experimental import pallas as pl
from jax.experimental.pallas import tpu as pltpu
from jax.sharding import PartitionSpec as P

B = 4096
C8 = 8


def trig_pair(first_count, second_count, stride_len, full_len):
    left = np.arange(first_count)[:, None]
    right = np.arange(second_count)[None, :]
    phases = (left * right * stride_len) % full_len
    angles = phases.astype(np.float64) * (2.0 * math.pi / full_len)
    return np.cos(angles).astype(np.float32), np.sin(angles).astype(np.float32)


def tables(rows, cols):
    full = rows * cols
    half = rows // 2
    cp, sp = trig_pair(rows, rows, cols, full)
    ct, st = trig_pair(rows, cols, 1, full)
    cq, sq = trig_pair(cols, cols, rows, full)
    eye = np.eye(C8, dtype=np.float32)
    row_fwd = np.kron(np.concatenate([cp[: half + 1], -sp[1:half]], 0), eye)
    twice = np.where(np.arange(half + 1) % half == 0, 1.0, 2.0) / full
    back = np.concatenate([cp[half:, : half + 1] * twice, -sp[half:, 1:half] * twice[1:half]], 1)
    row_inv = np.kron(back, eye)
    col = np.concatenate([np.block([[cq, -sq], [sq, cq]]), np.block([[cq, sq], [-sq, cq]])], 1)
    bands = np.concatenate([row_fwd, row_inv, col], 0).astype(jnp.bfloat16)
    turn = np.repeat(np.concatenate([ct, st], 1)[: half + 1], C8, axis=0).astype(np.float32)
    return bands, turn


def dot(a, b):
    return jnp.dot(a, b, preferred_element_type=jnp.float32)


def local_kernel(due_ref, context_ref, near_ref, next_ref, far_ref, last_ref, bands_ref, turn_ref, out_ref):
    left_over, part = due_ref[0], due_ref[1]
    seq, parts, chans, q = context_ref.shape
    length = 2 * seq * C8
    kept = turn_ref.shape[0]
    row_fwd = bands_ref.at[pl.ds(0, length), :]
    row_inv = bands_ref.at[pl.ds(length, length // 2), :]
    col = bands_ref.at[pl.ds(length + length // 2, 2 * q), :]
    groups = chans // C8

    def narrow(value):
        return value.astype(jnp.bfloat16)

    def beside(values):
        return narrow(jnp.concatenate(values, 1))

    def below(values):
        return jnp.concatenate(values, 0)

    @pl.when(left_over != 0)
    def _():
        out_ref[...] = jnp.zeros_like(out_ref)

    @pl.when(left_over == 0)
    def _():
        ct, st = turn_ref[:, :q], turn_ref[:, q:]
        edge = jnp.zeros((C8, q), jnp.float32)

        def spectra(head):
            turned = []
            for i in range(groups):
                value = head[:, i * q : (i + 1) * q]
                re = value[:kept]
                im = below([edge, value[kept:], edge])
                turned.append(jnp.concatenate([re * ct + im * st, im * ct - re * st], 1))
            return dot(narrow(below(turned)), col[:, : 2 * q])

        for step, filter_ref in enumerate((near_ref, next_ref, far_ref, last_ref)):
            place = lax.rem(part + step, parts)
            taps, signal = [], []
            for i in range(groups):
                rows = slice(i * C8, (i + 1) * C8)
                halves = [filter_ref[:, rows, h * q : (h + 1) * q].astype(jnp.float32) for h in range(2)]
                taps.append(jnp.stack(halves, 1).reshape(length, q))
                signal.append(context_ref[:, place, rows, :].astype(jnp.float32).reshape(seq * C8, q))
            filt = spectra(dot(row_fwd[...], beside(taps)))
            spec = spectra(dot(row_fwd[:, : seq * C8], beside(signal)))
            f_re, f_im, s_re, s_im = filt[:, :q], filt[:, q:], spec[:, :q], spec[:, q:]
            u = dot(beside([s_re * f_re - s_im * f_im, s_re * f_im + s_im * f_re]), col[:, 2 * q :])
            back = []
            for i in range(groups):
                u_re, u_im = u[i * kept : (i + 1) * kept, :q], u[i * kept : (i + 1) * kept, q:]
                v_im = u_re * st + u_im * ct
                back.append(below([u_re * ct - u_im * st, v_im[C8 : kept - C8]]))
            tail = dot(row_inv[...], beside(back))
            for i in range(groups):
                value = tail[:, i * q : (i + 1) * q].reshape(seq, C8, q)
                out_ref[:, place, i * C8 : (i + 1) * C8, :] = narrow(value)


def per_device(consts, parts, context, filters, lengths):
    seq, reqs = lax.axis_size("seq"), lax.axis_size("req")
    home = lax.axis_index("req")
    part = home % parts
    q = context.shape[2]
    chans = context.shape[1] // seq // parts
    left_over = lax.dynamic_index_in_dim(lengths, home, 0, keepdims=False) % B

    mine = lax.dynamic_index_in_dim(filters.reshape(seq, parts, chans, 2 * q), part, 1, keepdims=False)
    near = lax.all_to_all(mine, "seq", split_axis=0, concat_axis=0)
    context, near = lax.optimization_barrier((context, near))
    got = lax.all_to_all(context.reshape(seq, parts * chans, q), "seq", split_axis=0, concat_axis=0)
    rest = []
    for step in range(1, parts):
        hop = step if 2 * step <= parts else step - parts
        rest.append(lax.ppermute(near, "req", [((r + hop) % reqs, r) for r in range(reqs)]))

    smem = pl.BlockSpec(memory_space=pltpu.SMEM)
    vmem = pl.BlockSpec(memory_space=pltpu.VMEM)
    out = pl.pallas_call(
        local_kernel,
        out_shape=jax.ShapeDtypeStruct((seq, parts, chans, q), jnp.bfloat16),
        in_specs=[smem] + [vmem] * (1 + parts + 2),
        out_specs=vmem,
        compiler_params=pltpu.CompilerParams(vmem_limit_bytes=48 << 20),
        name="transform",
    )(jnp.stack([left_over, part]), got.reshape(seq, parts, chans, q), near, *rest, *consts)
    done = lax.all_to_all(out.reshape(seq, parts * chans, q), "seq", split_axis=0, concat_axis=0)
    return done.reshape(context.shape)


def solution(mesh):
    seq = mesh.shape["seq"]
    parts = 4
    consts = tables(2 * seq, B // seq)
    spec = P("req", "chan", "seq")
    return jax.shard_map(
        functools.partial(per_device, consts, parts),
        mesh=mesh,
        in_specs=(spec, P("chan", "seq"), P()),
        out_specs=spec,
        check_vma=False,
    )
```

time: 74.4 us -> 88.4 us (1.19)
  blocking collectives: 24.4 us -> 52 us
  waiting for transfers between devices: 27.2 us -> 11.7 us
  between operations: 0.03 us -> 1.94 us
  local copies, waits for them, and re-layouts: 1.53 us -> 3.33 us
  starting transfers between devices: 14.9 us -> 13.8 us
    all_to_all x1 -> x2, blocking collectives: 24.4 us -> 52 us  [the longest x1 26.3 us: per_device(): lax.all_to_all(out.reshape(seq, parts * chans, q), 'seq', split_axis=0, c...]
    all_to_all x1, waiting for transfers between devices: 27.2 us -> 0.01 us  [per_device(): lax.all_to_all(context.reshape(seq, parts * chans, q), 'seq', split_axis=...]
    ppermute x0 -> x3, waiting for transfers between devices: none -> 11.7 us  [per_device(): lax.ppermute(near, 'req', [((r + hop) % reqs, r) for r in range(reqs)])]
    all_to_all x1, starting transfers between devices: 14.9 us -> 4.22 us  [per_device(): lax.all_to_all(context.reshape(seq, parts * chans, q), 'seq', split_axis=...]
    ppermute x0 -> x3, starting transfers between devices: none -> 9.54 us  [per_device(): lax.ppermute(near, 'req', [((r + hop) % reqs, r) for r in range(reqs)])]
    unnamed x7 -> x9, local copies, waits for them, and re-layouts: 1.45 us -> 2.68 us
    pallas_call x2 -> x1, Pallas kernels: 5.95 us -> 5.15 us  [per_device(): pl.pallas_call(local_kernel, out_shape=jax.ShapeDtypeStruct((seq, parts,...]
  transfers between devices with their start and end apart: 1 -> 4, of which waited for: 1 -> 2; matrix products, arithmetic and copies ran while one was open for 0% -> 1% of each run, Pallas kernels for 0% -> 0%
where the time goes in v4:
time: 88.4 us; the launch traced here: 88 us
  blocking collectives  52 us (59%)
  starting transfers between devices  13.8 us (16%)
  waiting for transfers between devices  11.7 us (13%)
  Pallas kernels  5.15 us (6%)
  local copies, waits for them, and re-layouts  3.33 us (4%)
  between operations  1.94 us (2%)
    all_to_all x1, blocking collectives, per_device(): lax.all_to_all(out.reshape(seq, parts * chans, q), 'seq', split_axis=0, c...  26.3 us
    all_to_all x1, blocking collectives, per_device(): near = lax.all_to_all(mine, 'seq', split_axis=0, concat_axis=0)  25.8 us
    ppermute x3, waiting for transfers between devices, per_device(): lax.ppermute(near, 'req', [((r + hop) % reqs, r) for r in range(reqs)])  11.7 us
    ppermute x3, starting transfers between devices, per_device(): lax.ppermute(near, 'req', [((r + hop) % reqs, r) for r in range(reqs)])  9.54 us
    pallas_call x1, Pallas kernels, per_device(): pl.pallas_call(local_kernel, out_shape=jax.ShapeDtypeStruct((seq, parts,...  5.15 us
    all_to_all x1, starting transfers between devices, per_device(): lax.all_to_all(context.reshape(seq, parts * chans, q), 'seq', split_axis=...  4.22 us
    unnamed x9, local copies, waits for them, and re-layouts  2.68 us
  transfers between devices with their start and end apart: 4, of which 2 were waited for; matrix products, arithmetic and copies ran while one was open for 1% of the time, Pallas kernels for 0%

profile of v4, /device:TPU:16, one launch (start us, length us, event | category | flops | bytes accessed | tf_op | source)
XLA Modules:
  0.0 88.0 jit_solution(15655545821867779492)
XLA Ops:
  0.0 0.0 copy-start
  0.0 1.2 %copy-done = bf16[2048,256]{1,0:T(8,128)(2,1)S(1)} copy-done((bf16[2048,256]{1,0:T(8,128)(2,1)S(1)}, bf16[2048,256]{1,0:T(8,128)(2,1)}, u32[]{:S(2)}) %copy-start) | copy-done | bytes 1048600
  1.2 0.0 copy-start.1
  1.2 25.8 %all_to_all.15.near_ref = bf16[32,16,256]{2,1,0:T(8,128)(2,1)S(1)} all-to-all(bf16[32,16,256]{2,1,0:T(8,128)(2,1)S(1)} %dynamic-slice_bitcast_fusion), channel_id=1, replica_groups=mesh['seq'=32,'req'=8,'chan'=2] {'seq'}, dimensions={0} | all-to-all | bytes 524288 | tf_op jit(solution)/shard_map/all_to_all | solution.py:114
  27.0 0.0 copy-start.2
  27.0 4.2 %all-to-all-start.1 = ((bf16[32,64,128]{2,1,0:T(8,128)(2,1)}), bf16[32,64,128]{2,1,0:T(8,128)(2,1)S(1)}, u32[]{:S(2)}, u32[]{:S(2)}) async-start(bf16[32,64,128]{2,1,0:T(8,128)(2,1)} %bitcast.16), calls=%async_computation.1 | async-start | bytes 1048576 | tf_op jit(solution)/shard_map/all_to_all | solution.py:116
  31.3 3.5 %collective-permute-start.2 = (bf16[32,16,256]{2,1,0:T(8,128)(2,1)S(1)}, bf16[32,16,256]{2,1,0:T(8,128)(2,1)S(1)}, u32[]{:S(2)}, u32[]{:S(2)}) collective-permute-start(bf16[32,16,256]{2,1,0:T(8,128)(2,1)S(1)} %all_to_all.15.near_ref), channel_id=1, source_target_pairs={{14,0},{0,2},{2,4},{4,6},{6,8},{8,10},{10,12},{12,14},{15,1},{1,3}... | collective-permute-start | bytes 786440 | tf_op jit(solution)/shard_map/ppermute | solution.py:120
  34.8 2.2 %collective-permute-start.1 = (bf16[32,16,256]{2,1,0:T(8,128)(2,1)S(1)}, bf16[32,16,256]{2,1,0:T(8,128)(2,1)}, u32[]{:S(2)}, u32[]{:S(2)}) collective-permute-start(bf16[32,16,256]{2,1,0:T(8,128)(2,1)S(1)} %all_to_all.15.near_ref), channel_id=1, source_target_pairs={{4,0},{6,2},{8,4},{10,6},{12,8},{14,10},{0,12},{2,14},{5,1},{7,3},... | collective-permute-start | bytes 786440 | tf_op jit(solution)/shard_map/ppermute | solution.py:120
  37.0 3.8 %collective-permute-start = (bf16[32,16,256]{2,1,0:T(8,128)(2,1)S(1)}, bf16[32,16,256]{2,1,0:T(8,128)(2,1)}, u32[]{:S(2)}, u32[]{:S(2)}) collective-permute-start(bf16[32,16,256]{2,1,0:T(8,128)(2,1)S(1)} %all_to_all.15.near_ref), channel_id=1, source_target_pairs={{2,0},{4,2},{6,4},{8,6},{10,8},{12,10},{14,12},{0,14},{3,1},{5,3},... | collective-permute-start | bytes 786440 | tf_op jit(solution)/shard_map/ppermute | solution.py:120
  40.8 0.0 copy-start.3
  40.8 0.6 copy-done.3
  41.5 0.6 dynamic_slice.8
  44.0 0.1 pad_add_fusion.due_ref
  44.1 0.0 collective-permute-done.2.last_ref
  44.1 8.9 %collective-permute-done.1.far_ref = bf16[32,16,256]{2,1,0:T(8,128)(2,1)} collective-permute-done((bf16[32,16,256]{2,1,0:T(8,128)(2,1)S(1)}, bf16[32,16,256]{2,1,0:T(8,128)(2,1)}, u32[]{:S(2)}, u32[]{:S(2)}) %collective-permute-start.1) | collective-permute-done | bytes 262176 | tf_op jit(solution)/shard_map/ppermute | solution.py:120
  53.0 2.8 %collective-permute-done.next_ref = bf16[32,16,256]{2,1,0:T(8,128)(2,1)} collective-permute-done((bf16[32,16,256]{2,1,0:T(8,128)(2,1)S(1)}, bf16[32,16,256]{2,1,0:T(8,128)(2,1)}, u32[]{:S(2)}, u32[]{:S(2)}) %collective-permute-start) | collective-permute-done | bytes 262176 | tf_op jit(solution)/shard_map/ppermute | solution.py:120
  55.8 0.0 all-to-all-done.1
  55.8 0.0 copy-done.1
  55.8 0.0 copy-done.2
  55.8 5.2 %transform.1 = bf16[32,4,16,128]{3,2,1,0:T(8,128)(2,1)S(1)} custom-call(s32[2]{0:T(128)S(1)} %pad_add_fusion.due_ref, bf16[32,4,16,128]{3,2,1,0:T(8,128)(2,1)S(1)} %bitcast.13, bf16[32,16,256]{2,1,0:T(8,128)(2,1)S(1)} %all_to_all.15.near_ref, bf16[32,16,256]{2,1,0:T(8,128)(2,1)} %collective-permute-done.next_ref, ...), custom_call_target="tpu_custom_call" | custom-call | tf_op jit(solution)/shard_map/transform/pallas_call | solution.py:124
  60.9 26.3 %all_to_all.16 = bf16[32,64,128]{2,1,0:T(8,128)(2,1)S(1)} all-to-all(bf16[32,64,128]{2,1,0:T(8,128)(2,1)S(1)} %bitcast.14), channel_id=1, replica_groups=mesh['seq'=32,'req'=8,'chan'=2] {'seq'}, dimensions={0} | all-to-all | bytes 1048576 | tf_op jit(solution)/shard_map/all_to_all | solution.py:132
  87.2 0.8 copy.9
  (1 shorter events, 0.0 us)
Async XLA Ops:
  0.0 1.2 %copy-start = (bf16[2048,256]{1,0:T(8,128)(2,1)S(1)}, bf16[2048,256]{1,0:T(8,128)(2,1)}, u32[]{:S(2)}) copy-start(bf16[2048,256]{1,0:T(8,128)(2,1)} %param.6) | copy-start | bytes 3145732
  1.2 54.5 %copy-start.1 = (bf16[1024,512]{1,0:T(8,128)(2,1)S(1)}, bf16[1024,512]{1,0:T(8,128)(2,1)}, u32[]{:S(2)}) copy-start(bf16[1024,512]{1,0:T(8,128)(2,1)} %constant.42.clone.bands_ref) | copy-start | bytes 3145732
  27.0 28.7 %copy-start.2 = (f32[264,256]{1,0:T(8,128)S(1)}, f32[264,256]{1,0:T(8,128)}, u32[]{:S(2)}) copy-start(f32[264,256]{1,0:T(8,128)} %constant.43.clone.turn_ref) | copy-start | bytes 811012
  27.0 28.7 %all-to-all-start.1 = ((bf16[32,64,128]{2,1,0:T(8,128)(2,1)}), bf16[32,64,128]{2,1,0:T(8,128)(2,1)S(1)}, u32[]{:S(2)}, u32[]{:S(2)}) async-start(bf16[32,64,128]{2,1,0:T(8,128)(2,1)} %bitcast.16), calls=%async_computation.1 | async-start | bytes 1048576 | tf_op jit(solution)/shard_map/all_to_all | solution.py:116
  31.3 12.8 %collective-permute-start.2 = (bf16[32,16,256]{2,1,0:T(8,128)(2,1)S(1)}, bf16[32,16,256]{2,1,0:T(8,128)(2,1)S(1)}, u32[]{:S(2)}, u32[]{:S(2)}) collective-permute-start(bf16[32,16,256]{2,1,0:T(8,128)(2,1)S(1)} %all_to_all.15.near_ref), channel_id=1, source_target_pairs={{14,0},{0,2},{2,4},{4,6},{6,8},{8,10},{10,12},{12,14},{15,1},{1,3}... | collective-permute-start | bytes 786440 | tf_op jit(solution)/shard_map/ppermute | solution.py:120
  34.8 18.2 %collective-permute-start.1 = (bf16[32,16,256]{2,1,0:T(8,128)(2,1)S(1)}, bf16[32,16,256]{2,1,0:T(8,128)(2,1)}, u32[]{:S(2)}, u32[]{:S(2)}) collective-permute-start(bf16[32,16,256]{2,1,0:T(8,128)(2,1)S(1)} %all_to_all.15.near_ref), channel_id=1, source_target_pairs={{4,0},{6,2},{8,4},{10,6},{12,8},{14,10},{0,12},{2,14},{5,1},{7,3},... | collective-permute-start | bytes 786440 | tf_op jit(solution)/shard_map/ppermute | solution.py:120
  37.0 18.7 %collective-permute-start = (bf16[32,16,256]{2,1,0:T(8,128)(2,1)S(1)}, bf16[32,16,256]{2,1,0:T(8,128)(2,1)}, u32[]{:S(2)}, u32[]{:S(2)}) collective-permute-start(bf16[32,16,256]{2,1,0:T(8,128)(2,1)S(1)} %all_to_all.15.near_ref), channel_id=1, source_target_pairs={{2,0},{4,2},{6,4},{8,6},{10,8},{12,10},{14,12},{0,14},{3,1},{5,3},... | collective-permute-start | bytes 786440 | tf_op jit(solution)/shard_map/ppermute | solution.py:120
  40.8 0.7 copy-start.3

commit v5 on v4

v5 whole, which is shorter than its diff:
```python
import functools
import math

import jax
import jax.numpy as jnp
import numpy as np
from jax import lax
from jax.experimental import pallas as pl
from jax.experimental.pallas import tpu as pltpu
from jax.sharding import PartitionSpec as P

B = 4096
C8 = 8


def trig_pair(first_count, second_count, stride_len, full_len):
    left = np.arange(first_count)[:, None]
    right = np.arange(second_count)[None, :]
    phases = (left * right * stride_len) % full_len
    angles = phases.astype(np.float64) * (2.0 * math.pi / full_len)
    return np.cos(angles).astype(np.float32), np.sin(angles).astype(np.float32)


def tables(rows, cols):
    full = rows * cols
    half = rows // 2
    cp, sp = trig_pair(rows, rows, cols, full)
    ct, st = trig_pair(rows, cols, 1, full)
    cq, sq = trig_pair(cols, cols, rows, full)
    eye = np.eye(C8, dtype=np.float32)
    row_fwd = np.kron(np.concatenate([cp[: half + 1], -sp[1:half]], 0), eye)
    twice = np.where(np.arange(half + 1) % half == 0, 1.0, 2.0) / full
    back = np.concatenate([cp[half:, : half + 1] * twice, -sp[half:, 1:half] * twice[1:half]], 1)
    row_inv = np.kron(back, eye)
    col = np.concatenate([np.block([[cq, -sq], [sq, cq]]), np.block([[cq, sq], [-sq, cq]])], 1)
    bands = np.concatenate([row_fwd, row_inv, col], 0).astype(jnp.bfloat16)
    turn = np.repeat(np.concatenate([ct, st], 1)[: half + 1], C8, axis=0).astype(np.float32)
    return bands, turn


def dot(a, b):
    return jnp.dot(a, b, preferred_element_type=jnp.float32)


PARTNERS = (1, 2, 6, 3, 7, 5, 4)


def pack_kernel(lengths_ref, home_ref, context_ref, filters_ref, sent_ref, plan_ref):
    reqs = lengths_ref.shape[0]
    chans, q = context_ref.shape[1:]
    home = home_ref[0]

    def put(row, group):
        for half in range(2):
            first = row + half * C8
            sent_ref[:, first : first + C8, :] = filters_ref[:, group * C8 : (group + 1) * C8, half * q : (half + 1) * q]

    own_due = lax.rem(lengths_ref[home], B) == 0

    @pl.when(own_due)
    def _():
        sent_ref[:, :chans, :] = context_ref[...]
        put(chans, 0)

    @pl.when(jnp.logical_not(own_due))
    def _():
        for group in range(1, chans // C8):
            put((group - 1) * 2 * C8, group)

    @pl.when(pl.program_id(0) == 0)
    def _():
        due = [jnp.where(lax.rem(lengths_ref[r], B) == 0, 1, 0) for r in range(reqs)]
        choice = jnp.int32(0)
        partner = home ^ PARTNERS[0]
        for i in reversed(range(len(PARTNERS))):
            v = PARTNERS[i]
            clash = functools.reduce(jnp.add, [due[r] * due[r ^ v] for r in range(reqs) if r < r ^ v])
            fits = clash == 0
            choice = jnp.where(fits, i, choice)
            partner = jnp.where(fits, home ^ v, partner)
        first_is_due = jnp.where(home < partner, own_due, jnp.logical_not(own_due))
        plan_ref[0] = choice
        plan_ref[1] = jnp.where(first_is_due, 0, 1)


def local_kernel(plan_ref, got_ref, bands_ref, turn_ref, out_ref):
    side = plan_ref[1]
    seq, _, _, q = got_ref.shape
    chans = out_ref.shape[2]
    length = 2 * seq * C8
    kept = turn_ref.shape[0]
    row_fwd = bands_ref.at[pl.ds(0, length), :]
    row_inv = bands_ref.at[pl.ds(length, length // 2), :]
    col = bands_ref.at[pl.ds(length + length // 2, 2 * q), :]
    ct, st = turn_ref[:, :q], turn_ref[:, q:]
    edge = jnp.zeros((C8, q), jnp.float32)
    wide = 2

    def narrow(value):
        return value.astype(jnp.bfloat16)

    def beside(values):
        return narrow(jnp.concatenate(values, 1))

    def below(values):
        return jnp.concatenate(values, 0)

    def rows_of(at, first, count):
        return got_ref[:, at, first : first + count, :].astype(jnp.float32).reshape(seq * count, q)

    def spectra(head):
        turned = []
        for i in range(wide):
            value = head[:, i * q : (i + 1) * q]
            re = value[:kept]
            im = below([edge, value[kept:], edge])
            turned.append(jnp.concatenate([re * ct + im * st, im * ct - re * st], 1))
        return dot(narrow(below(turned)), col[:, : 2 * q])

    out_ref[:, 1 - side, :, :] = jnp.zeros((seq, chans, q), jnp.bfloat16)
    for first in range(0, chans // C8, wide):
        taps, signal = [], []
        for group in range(first, first + wide):
            if group:
                taps.append(rows_of(1 - side, (group - 1) * 2 * C8, 2 * C8))
            else:
                taps.append(rows_of(side, chans, 2 * C8))
            signal.append(rows_of(side, group * C8, C8))
        filt = spectra(dot(row_fwd[...], beside(taps)))
        spec = spectra(dot(row_fwd[:, : seq * C8], beside(signal)))
        f_re, f_im, s_re, s_im = filt[:, :q], filt[:, q:], spec[:, :q], spec[:, q:]
        u = dot(beside([s_re * f_re - s_im * f_im, s_re * f_im + s_im * f_re]), col[:, 2 * q :])
        back = []
        for i in range(wide):
            u_re, u_im = u[i * kept : (i + 1) * kept, :q], u[i * kept : (i + 1) * kept, q:]
            v_im = u_re * st + u_im * ct
            back.append(below([u_re * ct - u_im * st, v_im[C8 : kept - C8]]))
        tail = dot(row_inv[...], beside(back))
        for i in range(wide):
            value = tail[:, i * q : (i + 1) * q].reshape(seq, C8, q)
            group = first + i
            out_ref[:, side, group * C8 : (group + 1) * C8, :] = narrow(value)


def exchange(choice, value, seq, reqs):
    def paired(v):
        groups = [[s * reqs + side for s in range(seq) for side in (r, r ^ v)] for r in range(reqs) if r < r ^ v]
        return lambda x: lax.all_to_all(x, ("seq", "req"), split_axis=0, concat_axis=0, axis_index_groups=groups)

    return lax.switch(choice, [paired(v) for v in PARTNERS], value)


def per_device(consts, context, filters, lengths):
    seq, reqs = lax.axis_size("seq"), lax.axis_size("req")
    home = lax.axis_index("req")
    q = context.shape[2]
    peers = 2 * seq
    chans = context.shape[1] // peers
    rows = chans + 2 * C8
    smem = pl.BlockSpec(memory_space=pltpu.SMEM)
    vmem = pl.BlockSpec(memory_space=pltpu.VMEM)

    steps = 2
    part = peers // steps
    sent, plan = pl.pallas_call(
        pack_kernel,
        out_shape=[jax.ShapeDtypeStruct((peers, rows, q), jnp.bfloat16), jax.ShapeDtypeStruct((2,), jnp.int32)],
        grid=(steps,),
        in_specs=[
            smem,
            smem,
            pl.BlockSpec((part, chans, q), lambda i: (i, 0, 0)),
            pl.BlockSpec((part, chans, 2 * q), lambda i: (i, 0, 0)),
        ],
        out_specs=[pl.BlockSpec((part, rows, q), lambda i: (i, 0, 0)), smem],
        name="pack",
    )(lengths, home[None], context.reshape(peers, chans, q), filters.reshape(peers, chans, 2 * q))
    got = exchange(plan[0], sent, seq, reqs)
    out = pl.pallas_call(
        local_kernel,
        out_shape=jax.ShapeDtypeStruct((seq, 2, chans, q), jnp.bfloat16),
        in_specs=[smem] + [vmem] * 3,
        out_specs=vmem,
        compiler_params=pltpu.CompilerParams(vmem_limit_bytes=48 << 20),
        name="transform",
    )(plan, got.reshape(seq, 2, rows, q), *consts)
    done = exchange(plan[0], out.reshape(peers, chans, q), seq, reqs)
    return done.reshape(context.shape)


def solution(mesh):
    seq = mesh.shape["seq"]
    consts = tables(2 * seq, B // seq)
    spec = P("req", "chan", "seq")
    return jax.shard_map(
        functools.partial(per_device, consts),
        mesh=mesh,
        in_specs=(spec, P("chan", "seq"), P()),
        out_specs=spec,
        check_vma=False,
    )
```

time: 88.4 us -> 78.3 us (0.89)
  the two profiles are of different devices: /device:TPU:16 before, /device:TPU:8 now
where the time goes in v5:
time: 78.3 us; the launch traced here: 78.1 us
  blocking collectives  71.8 us (92%)
  Pallas kernels  4.76 us (6%)
  local copies, waits for them, and re-layouts  1.4 us (2%)
    all_to_all x2, blocking collectives, paired(): lax.all_to_all(x, ('seq', 'req'), split_axis=0, concat_axis=0, axis_index...  71.8 us
    pallas_call x1, Pallas kernels, per_device(): pl.pallas_call(local_kernel, out_shape=jax.ShapeDtypeStruct((seq, 2, chan...  2.79 us
    pallas_call x1, Pallas kernels, per_device(): pl.pallas_call(pack_kernel, out_shape=[jax.ShapeDtypeStruct((peers, rows,...  1.96 us

profile of v5, /device:TPU:8, one launch (start us, length us, event | category | flops | bytes accessed | tf_op | source)
XLA Modules:
  0.0 78.1 jit_solution(11712954098109987146)
XLA Ops:
  0.0 2.0 %pack.1 = (bf16[64,48,128]{2,1,0:T(8,128)(2,1)S(1)}, s32[2]{0:T(128)}) custom-call(s32[8]{0:T(128)} %lengths_ref.1, s32[1]{0:T(128)} %bitcast.21.home_ref, bf16[64,32,128]{2,1,0:T(8,128)(2,1)} %bitcast.49, bf16[64,32,256]{2,1,0:T(8,128)(2,1)} %bitcast.48), custom_call_target="tpu_custom_call" | custom-call | tf_op jit(solution)/shard_map/pack/pallas_call | solution.py:165
  2.0 0.0 copy-start.2
  2.0 0.6 copy-done.2
  2.6 0.0 copy-start
  2.6 0.0 copy-start.1
  2.6 46.1 %conditional.2 = (bf16[32,2,48,128]{3,2,1,0:T(8,128)(2,1)S(1)}) conditional(s32[]{:T(128)} %bitcast.24, bf16[64,48,128]{2,1,0:T(8,128)(2,1)S(1)} %get-tuple-element.47, bf16[64,48,128]{2,1,0:T(8,128)(2,1)S(1)} %get-tuple-element.47, bf16[64,48,128]{2,1,0:T(8,128)(2,1)S(1)} %get-tuple-element.47, ...), branch_computations={%region_0.0_spmd, %region_1.0_spmd, %region_2.0_spmd, %region_3.0_... | conditional | bytes 1572872 | solution.py:150
  2.7 46.0 %all_to_all.61 = bf16[64,48,128]{2,1,0:T(8,128)(2,1)S(1)} all-to-all(bf16[64,48,128]{2,1,0:T(8,128)(2,1)S(1)} %param.5), channel_id=1, replica_groups={{0,10,16,26,32,42,48,58,64,74,80,90,96,106,112,122,128,138,144,154,160,..., dimensions={0} | all-to-all | bytes 1572864 | tf_op jit(solution)/shard_map/cond/branch_5_fun/all_to_all | solution.py:148
  48.7 0.0 copy-done
  48.7 0.0 copy-done.1
  48.7 2.8 %transform.1 = bf16[32,2,32,128]{3,2,1,0:T(8,128)(2,1)S(1)} custom-call(s32[2]{0:T(128)S(1)} %copy-done.2, bf16[32,2,48,128]{3,2,1,0:T(8,128)(2,1)S(1)} %get-tuple-element.56.got_ref, bf16[1024,512]{1,0:T(8,128)(2,1)S(1)} %copy-done, f32[264,256]{1,0:T(8,128)S(1)} %copy-done.1), custom_call_target="tpu_custom_call" | custom-call | tf_op jit(solution)/shard_map/transform/pallas_call | solution.py:179
  51.5 25.8 %conditional.3 = (bf16[1,2048,128]{2,1,0:T(8,128)(2,1)S(1)}) conditional(s32[]{:T(128)} %bitcast.24, bf16[32,2,32,128]{3,2,1,0:T(8,128)(2,1)S(1)} %transform.1, bf16[32,2,32,128]{3,2,1,0:T(8,128)(2,1)S(1)} %transform.1, bf16[32,2,32,128]{3,2,1,0:T(8,128)(2,1)S(1)} %transform.1, ...), branch_computations={%region_7.0_spmd, %region_8.0_spmd, %region_9.0_spmd, %region_10.0... | conditional | bytes 1048584 | solution.py:150
  51.6 25.7 %all_to_all.68 = bf16[64,32,128]{2,1,0:T(8,128)(2,1)S(1)} all-to-all(bf16[64,32,128]{2,1,0:T(8,128)(2,1)S(1)} %bitcast.32), channel_id=1, replica_groups={{0,10,16,26,32,42,48,58,64,74,80,90,96,106,112,122,128,138,144,154,160,..., dimensions={0} | all-to-all | bytes 1048576 | tf_op jit(solution)/shard_map/cond/branch_5_fun/all_to_all | solution.py:148
  77.3 0.8 %copy.28 = bf16[1,2048,128]{2,1,0:T(8,128)(2,1)} copy(bf16[1,2048,128]{2,1,0:T(8,128)(2,1)S(1)} %get-tuple-element.48) | data formatting | bytes 1048576
Async XLA Ops:
  2.0 0.6 copy-start.2
  2.6 46.1 %copy-start = (bf16[1024,512]{1,0:T(8,128)(2,1)S(1)}, bf16[1024,512]{1,0:T(8,128)(2,1)}, u32[]{:S(2)}) copy-start(bf16[1024,512]{1,0:T(8,128)(2,1)} %constant.16.clone.bands_ref) | copy-start | bytes 3145732
  2.6 46.1 %copy-start.1 = (f32[264,256]{1,0:T(8,128)S(1)}, f32[264,256]{1,0:T(8,128)}, u32[]{:S(2)}) copy-start(f32[264,256]{1,0:T(8,128)} %constant.17.clone.turn_ref) | copy-start | bytes 811012

commit v6 on v5

--- a/solution.py
+++ b/solution.py
@@ -42,7 +42,16 @@
     return jnp.dot(a, b, preferred_element_type=jnp.float32)
 
 
-PARTNERS = (1, 2, 6, 3, 7, 5, 4)
+PAIRINGS = (
+    ((0, 1), (2, 3), (4, 5), (6, 7)),
+    ((0, 3), (1, 2), (4, 7), (5, 6)),
+    ((0, 7), (1, 2), (3, 4), (5, 6)),
+    ((0, 7), (1, 6), (2, 5), (3, 4)),
+    ((0, 1), (2, 7), (3, 6), (4, 5)),
+    ((0, 6), (1, 3), (2, 4), (5, 7)),
+    ((0, 2), (1, 7), (3, 5), (4, 6)),
+    ((0, 5), (1, 4), (2, 3), (6, 7)),
+)
 
 
 def pack_kernel(lengths_ref, home_ref, context_ref, filters_ref, sent_ref, plan_ref):
@@ -70,15 +79,15 @@
     @pl.when(pl.program_id(0) == 0)
     def _():
         due = [jnp.where(lax.rem(lengths_ref[r], B) == 0, 1, 0) for r in range(reqs)]
-        choice = jnp.int32(0)
-        partner = home ^ PARTNERS[0]
-        for i in reversed(range(len(PARTNERS))):
-            v = PARTNERS[i]
-            clash = functools.reduce(jnp.add, [due[r] * due[r ^ v] for r in range(reqs) if r < r ^ v])
-            fits = clash == 0
-            choice = jnp.where(fits, i, choice)
-            partner = jnp.where(fits, home ^ v, partner)
-        first_is_due = jnp.where(home < partner, own_due, jnp.logical_not(own_due))
+        choice, partners = jnp.int32(0), jnp.int32(0)
+        for i in reversed(range(len(PAIRINGS))):
+            clash = functools.reduce(jnp.add, [due[a] * due[b] for a, b in PAIRINGS[i]])
+            code = sum((b << 4 * a) + (a << 4 * b) for a, b in PAIRINGS[i])
+            code -= (code >> 31) << 32
+            choice = jnp.where(clash == 0, i, choice)
+            partners = jnp.where(clash == 0, jnp.int32(code), partners)
+        partner = lax.shift_right_logical(partners, 4 * home) & 15
+        first_is_due = (home < partner) == own_due
         plan_ref[0] = choice
         plan_ref[1] = jnp.where(first_is_due, 0, 1)
 
@@ -143,11 +152,11 @@
 
 
 def exchange(choice, value, seq, reqs):
-    def paired(v):
-        groups = [[s * reqs + side for s in range(seq) for side in (r, r ^ v)] for r in range(reqs) if r < r ^ v]
+    def paired(pairs):
+        groups = [[s * reqs + side for s in range(seq) for side in pair] for pair in pairs]
         return lambda x: lax.all_to_all(x, ("seq", "req"), split_axis=0, concat_axis=0, axis_index_groups=groups)
 
-    return lax.switch(choice, [paired(v) for v in PARTNERS], value)
+    return lax.switch(choice, [paired(pairs) for pairs in PAIRINGS], value)
 
 
 def per_device(consts, context, filters, lengths):

time: 78.3 us -> 70.7 us (0.903)
  the two profiles are of different devices: /device:TPU:8 before, /device:TPU:2 now
where the time goes in v6:
time: 70.7 us; the launch traced here: 70.5 us
  blocking collectives  64.2 us (91%)
  Pallas kernels  4.77 us (7%)
  local copies, waits for them, and re-layouts  1.4 us (2%)
    all_to_all x2, blocking collectives, paired(): lax.all_to_all(x, ('seq', 'req'), split_axis=0, concat_axis=0, axis_index...  64.2 us
    pallas_call x1, Pallas kernels, per_device(): pl.pallas_call(local_kernel, out_shape=jax.ShapeDtypeStruct((seq, 2, chan...  2.8 us
    pallas_call x1, Pallas kernels, per_device(): pl.pallas_call(pack_kernel, out_shape=[jax.ShapeDtypeStruct((peers, rows,...  1.97 us

profile of v6, /device:TPU:2, one launch (start us, length us, event | category | flops | bytes accessed | tf_op | source)
XLA Modules:
  0.0 70.5 jit_solution(1085965766565922795)
XLA Ops:
  0.0 2.0 %pack.1 = (bf16[64,48,128]{2,1,0:T(8,128)(2,1)S(1)}, s32[2]{0:T(128)}) custom-call(s32[8]{0:T(128)} %lengths_ref.1, s32[1]{0:T(128)} %bitcast.24.home_ref, bf16[64,32,128]{2,1,0:T(8,128)(2,1)} %bitcast.55, bf16[64,32,256]{2,1,0:T(8,128)(2,1)} %bitcast.54), custom_call_target="tpu_custom_call" | custom-call | tf_op jit(solution)/shard_map/pack/pallas_call | solution.py:174
  2.0 0.0 copy-start.2
  2.0 0.6 copy-done.2
  2.6 0.0 copy-start
  2.6 0.0 copy-start.1
  2.6 39.2 %conditional.2 = (bf16[32,2,48,128]{3,2,1,0:T(8,128)(2,1)S(1)}) conditional(s32[]{:T(128)} %bitcast.27, bf16[64,48,128]{2,1,0:T(8,128)(2,1)S(1)} %get-tuple-element.52, bf16[64,48,128]{2,1,0:T(8,128)(2,1)S(1)} %get-tuple-element.52, bf16[64,48,128]{2,1,0:T(8,128)(2,1)S(1)} %get-tuple-element.52, ...), branch_computations={%region_0.0_spmd, %region_1.0_spmd, %region_2.0_spmd, %region_3.0_... | conditional | bytes 1572872 | solution.py:159
  2.7 39.2 %all_to_all.65 = bf16[64,48,128]{2,1,0:T(8,128)(2,1)S(1)} all-to-all(bf16[64,48,128]{2,1,0:T(8,128)(2,1)S(1)} %param.1), channel_id=1, replica_groups={{0,6,16,22,32,38,48,54,64,70,80,86,96,102,112,118,128,134,144,150,160,1..., dimensions={0} | all-to-all | bytes 1572864 | tf_op jit(solution)/shard_map/cond/branch_1_fun/all_to_all | solution.py:157
  41.8 0.0 copy-done
  41.8 0.0 copy-done.1
  41.8 2.8 %transform.1 = bf16[32,2,32,128]{3,2,1,0:T(8,128)(2,1)S(1)} custom-call(s32[2]{0:T(128)S(1)} %copy-done.2, bf16[32,2,48,128]{3,2,1,0:T(8,128)(2,1)S(1)} %get-tuple-element.62.got_ref, bf16[1024,512]{1,0:T(8,128)(2,1)S(1)} %copy-done, f32[264,256]{1,0:T(8,128)S(1)} %copy-done.1), custom_call_target="tpu_custom_call" | custom-call | tf_op jit(solution)/shard_map/transform/pallas_call | solution.py:188
  44.6 25.1 %conditional.3 = (bf16[1,2048,128]{2,1,0:T(8,128)(2,1)S(1)}) conditional(s32[]{:T(128)} %bitcast.27, bf16[32,2,32,128]{3,2,1,0:T(8,128)(2,1)S(1)} %transform.1, bf16[32,2,32,128]{3,2,1,0:T(8,128)(2,1)S(1)} %transform.1, bf16[32,2,32,128]{3,2,1,0:T(8,128)(2,1)S(1)} %transform.1, ...), branch_computations={%region_8.0_spmd, %region_9.0_spmd, %region_10.0_spmd, %region_11.... | conditional | bytes 1048584 | solution.py:159
  44.7 25.1 %all_to_all.73 = bf16[64,32,128]{2,1,0:T(8,128)(2,1)S(1)} all-to-all(bf16[64,32,128]{2,1,0:T(8,128)(2,1)S(1)} %bitcast.31), channel_id=1, replica_groups={{0,6,16,22,32,38,48,54,64,70,80,86,96,102,112,118,128,134,144,150,160,1..., dimensions={0} | all-to-all | bytes 1048576 | tf_op jit(solution)/shard_map/cond/branch_1_fun/all_to_all | solution.py:157
  69.7 0.8 %copy.31 = bf16[1,2048,128]{2,1,0:T(8,128)(2,1)} copy(bf16[1,2048,128]{2,1,0:T(8,128)(2,1)S(1)} %get-tuple-element.53) | data formatting | bytes 1048576
Async XLA Ops:
  2.0 0.6 copy-start.2
  2.6 39.2 %copy-start = (bf16[1024,512]{1,0:T(8,128)(2,1)S(1)}, bf16[1024,512]{1,0:T(8,128)(2,1)}, u32[]{:S(2)}) copy-start(bf16[1024,512]{1,0:T(8,128)(2,1)} %constant.16.clone.bands_ref) | copy-start | bytes 3145732
  2.6 39.2 %copy-start.1 = (f32[264,256]{1,0:T(8,128)S(1)}, f32[264,256]{1,0:T(8,128)}, u32[]{:S(2)}) copy-start(f32[264,256]{1,0:T(8,128)} %constant.17.clone.turn_ref) | copy-start | bytes 811012
